TPU v7x, 256 devices: a whole 4x4x8 slice. The times are simulated.
256 devices in a mesh: ctx: 32 (over z, y_hi, core), head: 8 (over y_lo, x).
Axes of the slice: x: 4, y: 4 (y_hi: 2, y_lo: 2; y = y_hi * 2 + y_lo), z: 8, core: 2. Of those that a mesh axis runs over, the one named last changes fastest.
Arguments:
- queries: bfloat16 [16384, 3072], P(('ctx', 'head')), may hold values from -6 to 6
- keys: bfloat16 [16384, 3072], P(('ctx', 'head')), may hold values from -6 to 6
- values: bfloat16 [16384, 3072], P(('ctx', 'head')), may hold values from -6 to 6
- span_tiles: int32 [4], replicated, may hold values from 1 to 48, 128 in all
Outputs:
- attended: bfloat16 [16384, 3072], P(('ctx', 'head'))
Inputs may be any that keep to these rules, and one draw needn't show every extreme that they name: `span_tiles`: the entries sum to 128; the longest span has exactly 48 tiles.
All inputs are finite; a program needn't handle non-finite values.
Results may differ from a plain program's by a relative error of at most 0.0075.
Values may be sent and summed in bfloat16 or wider, within the bound.
No kernel may reach another device: no remote copies, remote signals or barrier semaphores. Data moves between devices by JAX's collectives and lax.ppermute only.
A program may use at most 128 MiB of HBM per device.

v0:
```python
import functools

import jax
import jax.numpy as jnp
from jax import lax
from jax.experimental import pallas as pl
from jax.experimental.pallas import tpu as pltpu
from jax.sharding import Mesh, PartitionSpec as P

HD = 128
TILE = 128
SPANS = 4
Z, YH, CORES, YL, X = 8, 2, 2, 2, 4
Y = YH * YL
TOK = 64
HALF = TOK // 2
HEADS_HERE = 3
QT = Y * TOK
KT = X * TOK
CHUNKS = Z * CORES
GROUP = 4
VROWS = HD + 16
LOW = -1e30
FLOOR = -1e20
FACTOR = HD ** (-0.5) * 1.4426950408889634
ALL = ("z", "yh", "c", "yl", "x")


def pack_kernel(q_ref, k_ref, v_ref, most, rest):
    for plane in range(Z):
        for core in range(CORES):
            to = plane * CORES + core
            half = slice(core * HALF, (core + 1) * HALF)
            shared = slice(plane * HEADS_HERE * HD, (plane * HEADS_HERE + 1) * HD)
            lo = (plane * HEADS_HERE + 1 + core) * HD
            own = slice(lo, lo + HD)
            most[to, 0:TOK, :] = k_ref[:, own]
            most[to, TOK:2 * TOK, :] = v_ref[:, own]
            most[to, 2 * TOK:3 * TOK, :] = q_ref[:, own]
            most[to, 3 * TOK:3 * TOK + HALF, :] = q_ref[half, shared]
            rest[to, 0:HALF, :] = k_ref[half, shared]
            rest[to, HALF:TOK, :] = v_ref[half, shared]


def pack(queries, keys, values):
    return pl.pallas_call(
        pack_kernel,
        out_shape=[
            jax.ShapeDtypeStruct((CHUNKS, 3 * TOK + HALF, HD), jnp.bfloat16),
            jax.ShapeDtypeStruct((CHUNKS, TOK, HD), jnp.bfloat16),
        ],
        name="pack",
    )(queries, keys, values)


def unpack_kernel(ref, out):
    for plane in range(Z):
        for core in range(CORES):
            at = plane * CORES + core
            lo = (plane * HEADS_HERE + 1 + core) * HD
            out[:, lo:lo + HD] = ref[at, 0:TOK, :]
            lo = plane * HEADS_HERE * HD
            out[core * HALF:(core + 1) * HALF, lo:lo + HD] = ref[at, TOK:TOK + HALF, :]


def unpack(parts):
    return pl.pallas_call(
        unpack_kernel,
        out_shape=jax.ShapeDtypeStruct((TOK, Z * HEADS_HERE * HD), jnp.bfloat16),
        name="unpack",
    )(parts)


def attend_kernel(shared, planes, join, span_tiles, *refs):
    qs, refs = refs[:Y], refs[Y:]
    mine, refs = (refs[:CORES], refs[CORES:]) if shared else (refs[:X], refs[X:])
    o_refs, refs = refs[:Y], refs[Y:]
    k_scr, v_scr, s_scr, q_scr, limit_scr, acc_scr, top_scr, steps, q_in, v_in, o_scr, sems = refs
    x = lax.axis_index("x")
    y = lax.axis_index("yh") * YL + lax.axis_index("yl")
    bounds = [span_tiles[0] * TILE]
    for s in range(1, SPANS):
        bounds.append(bounds[-1] + span_tiles[s] * TILE)

    copies = [[], [], []]

    def fetch(kind, source, target):
        copy = pltpu.make_async_copy(source, target, sems.at[sum(map(len, copies))])
        copy.start()
        copies[kind].append(copy)

    for d in range(Y):
        at = pl.ds(TOK, HALF) if shared else pl.ds(0, TOK)
        fetch(0, qs[d].at[:, at, :], q_in.at[d])
    size = HALF if shared else TOK
    for d in range(X):
        sources = [ref.at[(x + X - d) % X] for ref in mine] if shared else [mine[d]]
        for e, source in enumerate(sources):
            at = pl.ds(d * TOK + e * HALF, size)
            fetch(1, source.at[:, pl.ds(size, size), :], v_in.at[:, at, :])
            for twice in range(2):
                fetch(2, source.at[:, pl.ds(0, size), :], k_scr.at[:, at, pl.ds(twice * HD, HD)])

    tiles = planes // join
    wide = join * QT
    ones = jnp.ones((VROWS - HD, KT), jnp.bfloat16)
    y_off = (y // YL) * (TOK * CORES * YL * X) + (y % YL) * KT
    lane = lax.broadcasted_iota(jnp.int32, (1, QT), 1)
    rows = planes * TOK

    def chunk_start(j):
        return (j // CORES) * (TOK * 32) + (j % CORES) * (TOK * 8) + y_off

    def arrange_values(j, carry):
        v_scr[j, 0:HD, :] = v_in[j].T
        v_scr[j, HD:VROWS, :] = ones
        return carry

    def arrange_queries(t, whole):
        most = jnp.int32(0)
        for part in range(join):
            i = t * join + part
            parts = []
            for d in range(Y):
                if shared:
                    parts += [q_in[d, i * CORES + e] for e in range(CORES)]
                else:
                    parts.append(q_in[d, i])
            q = jnp.concatenate(parts, axis=0).astype(jnp.float32) * FACTOR
            high = q.astype(jnp.bfloat16)
            low = (q - high.astype(jnp.float32)).astype(jnp.bfloat16)
            at = slice(part * QT, (part + 1) * QT)
            q_scr[t, at, 0:HD] = high
            q_scr[t, at, HD:2 * HD] = low
            row = jnp.zeros((1, QT), jnp.int32)
            for block in range(QT // size):
                yq = (y + Y - (block * size) // TOK) % Y
                j = i * CORES + block % CORES if shared else i
                tok = (j // CORES) * (TOK * 32) + (yq // YL) * (TOK * 16) + (j % CORES) * (TOK * 8) + (yq % YL) * (TOK * 4) + x * TOK
                end = bounds[SPANS - 1]
                for s in range(SPANS - 2, -1, -1):
                    end = jnp.where(tok < bounds[s], bounds[s], end)
                most = jnp.maximum(most, end)
                row = jnp.where(lane >= block * size, end, row)
            limit_scr[t, 0:1, at] = row
        far = jnp.maximum(most - y_off, 0)
        rest = far % (TOK * 32)
        seen = (far // (TOK * 32)) * CORES + (rest > 0).astype(jnp.int32) + (rest > TOK * 8).astype(jnp.int32)
        count = jnp.maximum((seen + GROUP - 1) // GROUP, 1)
        steps[t] = count
        acc_scr[t] = jnp.zeros((VROWS, wide), jnp.float32)
        return whole + count

    for copy in copies[0]:
        copy.wait()
    rounds = lax.fori_loop(0, tiles, arrange_queries, jnp.int32(0))
    for copy in copies[1]:
        copy.wait()
    lax.fori_loop(0, CHUNKS, arrange_values, 0)
    for copy in copies[2]:
        copy.wait()

    def bias_rows(t, j):
        start = chunk_start(j)
        limit_row = limit_scr[t, 0:1, :]
        return [jnp.where(start + ((x + X - d) % X) * TOK < limit_row, 0.0, LOW) for d in range(X)]

    def produce(t, j, slot, best):
        s = lax.dot_general(k_scr[j], q_scr[t], (((1,), (1,)), ((), ())), preferred_element_type=jnp.float32)
        s_scr[slot] = s
        for d, bias in enumerate(bias_rows(t, j)):
            part = jnp.max(s[d * TOK:(d + 1) * TOK].reshape(TOK // 8, 8, wide), axis=0) + bias
            best = jnp.maximum(best, part)
        return best

    def consume(t, j, slot, top):
        s = s_scr[slot]
        ps = []
        for d, bias in enumerate(bias_rows(t, j)):
            ps.append(jnp.exp2(s[d * TOK:(d + 1) * TOK] - (top - bias)).astype(jnp.bfloat16))
        return jnp.concatenate(ps, axis=0)

    def step(_, state):
        t, n, best, old = state
        top = jnp.max(best, axis=0, keepdims=True)
        last = n + 1 >= steps[t]
        t2 = jnp.where(last, jnp.minimum(t + 1, tiles - 1), t)
        n2 = jnp.where(last, 0, n + 1)
        best = jnp.where(last, FLOOR, best)
        accum = acc_scr[t] * jnp.exp2(old - top)
        for g in range(GROUP):
            j = n * GROUP + g
            p = consume(t, j, g, top)
            best = produce(t2, n2 * GROUP + g, g, best)
            accum = accum + jnp.dot(v_scr[j], p, preferred_element_type=jnp.float32)
        acc_scr[t] = accum
        top_scr[t, 0:1, :] = top
        return t2, n2, best, jnp.where(last, FLOOR, top)

    best = jnp.full((8, wide), FLOOR, jnp.float32)
    for g in range(GROUP):
        best = produce(0, g, g, best)
    lax.fori_loop(0, rounds, step, (jnp.int32(0), jnp.int32(0), best, jnp.full((1, wide), FLOOR, jnp.float32)))
    stats = []
    for i in range(planes):
        t, at = i // join, slice(i % join * QT, (i % join + 1) * QT)
        total = acc_scr[t, HD:HD + 1, at]
        some = total > 0.0
        safe = jnp.where(some, total, 1.0)
        stats.append(jnp.where(some, top_scr[t, 0:1, at] + jnp.log2(safe), LOW))
        out = (acc_scr[t, 0:HD, at] * (1.0 / safe)).T.astype(jnp.bfloat16)
        for d in range(Y):
            o_scr[d, i * TOK:(i + 1) * TOK, :] = out[d * TOK:(d + 1) * TOK]
    lse = jnp.concatenate(stats, axis=0)
    high = lse.astype(jnp.bfloat16)
    lse = lse - high.astype(jnp.float32)
    middle = lse.astype(jnp.bfloat16)
    low = (lse - middle.astype(jnp.float32)).astype(jnp.bfloat16)
    for d in range(Y):
        at = slice(d * TOK, (d + 1) * TOK)
        first = jnp.concatenate([high[:, at], middle[:, at]], axis=1)
        second = jnp.concatenate([low[:, at], jnp.zeros((planes, HD - TOK), jnp.bfloat16)], axis=1)
        o_scr[d, rows:rows + 2 * planes, :] = jnp.concatenate([first, second], axis=0)
    out_copies = [pltpu.make_async_copy(o_scr.at[d], o_refs[d], sems.at[d]) for d in range(Y)]
    for copy in out_copies:
        copy.start()
    for copy in out_copies:
        copy.wait()


def attend(span_tiles, shared, qs, mine):
    planes = Z if shared else CHUNKS
    join = 2 if shared else 4
    tiles, wide = planes // join, join * QT
    pairs = planes * QT * CHUNKS * KT
    arrays = [*qs, *mine]
    return pl.pallas_call(
        functools.partial(attend_kernel, shared, planes, join),
        in_specs=[pl.BlockSpec(memory_space=pltpu.SMEM)] + [pl.BlockSpec(memory_space=pl.ANY)] * len(arrays),
        out_specs=[pl.BlockSpec(memory_space=pl.ANY)] * Y,
        out_shape=[jax.ShapeDtypeStruct((planes * (TOK + 2), HD), jnp.bfloat16)] * Y,
        scratch_shapes=[
            pltpu.VMEM((CHUNKS, KT, 2 * HD), jnp.bfloat16),
            pltpu.VMEM((CHUNKS, VROWS, KT), jnp.bfloat16),
            pltpu.VMEM((GROUP, KT, wide), jnp.float32),
            pltpu.VMEM((tiles, wide, 2 * HD), jnp.bfloat16),
            pltpu.VMEM((tiles, 8, wide), jnp.int32),
            pltpu.VMEM((tiles, VROWS, wide), jnp.float32),
            pltpu.VMEM((tiles, 8, wide), jnp.float32),
            pltpu.SMEM((tiles,), jnp.int32),
            pltpu.VMEM((Y, CHUNKS, HALF if shared else TOK, HD), jnp.bfloat16),
            pltpu.VMEM((CHUNKS, KT, HD), jnp.bfloat16),
            pltpu.VMEM((Y, planes * (TOK + 2), HD), jnp.bfloat16),
            pltpu.SemaphoreType.DMA((Y + 3 * X * (2 if shared else 1),)),
        ],
        compiler_params=pltpu.CompilerParams(vmem_limit_bytes=30 * 1024 * 1024),
        cost_estimate=pl.CostEstimate(flops=8 * pairs * HD, bytes_accessed=4 << 20, transcendentals=pairs),
        name="attend_shared" if shared else "attend_own",
    )(span_tiles, *arrays)


def turn(array, axis, size, by):
    return lax.ppermute(array, axis, [(i, (i + by) % size) for i in range(size)])


def after(array, *earlier):
    return lax.optimization_barrier((array, *earlier))[0]


def along_z(array):
    return lax.all_to_all(array, ("z", "c"), split_axis=0, concat_axis=0, tiled=True)


def combine(outs):
    tiles = outs[0].shape[0] // (TOK + 2)
    rows = tiles * TOK
    stats = []
    for item in outs:
        three = item[rows:].astype(jnp.float32)
        stats.append(three[:tiles, :TOK] + three[:tiles, TOK:] + three[tiles:, :TOK])
    top = jnp.maximum(jnp.maximum(stats[0], stats[1]), jnp.maximum(stats[2], stats[3]))
    weights = [jnp.exp2(item - top) for item in stats]
    total = weights[0] + weights[1] + weights[2] + weights[3]
    mixed = sum(
        (w / total)[:, :, None] * item[:rows].reshape(tiles, TOK, HD).astype(jnp.float32)
        for w, item in zip(weights, outs)
    )
    return mixed.astype(jnp.bfloat16).reshape(CHUNKS, -1, HD)


def body(queries, keys, values, span_tiles):
    def spread(array):
        return [turn(array, "x", X, d) for d in range(1, X)]

    def exchange(out):
        return [out[0]] + [turn(out[d], ("yh", "yl"), Y, -d) for d in range(1, Y)]

    most, rest = pack(queries, keys, values)
    most = along_z(most)
    rest = along_z(after(rest, most))
    mine = [most] + spread(most[:, :2 * TOK])
    q = most[:, 2 * TOK:]
    qs = [q] + [turn(q, ("yh", "yl"), Y, d) for d in range(1, Y - 1)]
    qs.append(turn(after(q, qs[1]), ("yh", "yl"), Y, Y - 1))
    mine2 = lax.all_to_all(
        jnp.broadcast_to(rest, (X, *rest.shape)), "x", split_axis=0, concat_axis=0, tiled=True
    )
    own_out = attend(span_tiles, False, qs, mine)
    others = lax.ppermute(after(mine2, own_out), "c", [(0, 1), (1, 0)])
    got = exchange(own_out)
    shared_out = attend(span_tiles, True, qs, [mine2, others])
    mixed = combine(after(got, shared_out))
    mixed2 = combine(exchange(shared_out))
    return unpack(along_z(jnp.concatenate([mixed, mixed2], axis=1)))


def solution(mesh):
    fine = Mesh(mesh.devices.reshape(Z, YH, CORES, YL, X), ALL)
    return jax.shard_map(
        body,
        mesh=fine,
        in_specs=(P(ALL, None), P(ALL, None), P(ALL, None), P()),
        out_specs=P(ALL, None),
        check_vma=False,
    )
```

profile of v0, /device:TPU:1, one launch (start us, length us, event | category | flops | bytes accessed | tf_op | source)
XLA Modules:
  0.0 151.4 jit_solution(9927287954938531940)
XLA Ops:
  0.0 2.4 %pack.1 = (bf16[16,224,128]{2,1,0:T(8,128)(2,1)}, bf16[16,64,128]{2,1,0:T(8,128)(2,1)}) custom-call(bf16[64,3072]{1,0:T(8,128)(2,1)} %q_ref.1, bf16[64,3072]{1,0:T(8,128)(2,1)} %k_ref.1, bf16[64,3072]{1,0:T(8,128)(2,1)} %v_ref.1), custom_call_target="tpu_custom_call" | custom-call | tf_op jit(solution)/shard_map/pack/pallas_call | solution.py:46
  2.4 35.7 %all_to_all.20.refs_4_ = bf16[16,224,128]{2,1,0:T(8,128)(2,1)S(1)} all-to-all(bf16[16,224,128]{2,1,0:T(8,128)(2,1)} %get-tuple-element.22), channel_id=1, replica_groups=mesh['z'=8,'yh'=2,'c'=2,'yl'=2,'x'=4] {'z','c'}, dimensions={0} | all-to-all | bytes 1835008 | tf_op jit(solution)/shard_map/all_to_all | solution.py:271
  38.2 1.4 collective-permute-start
  39.6 0.8 slice.169
  40.4 1.2 collective-permute-start.3
  41.6 2.5 %collective-permute-start.4 = (bf16[16,128,128]{2,1,0:T(8,128)(2,1)}, bf16[16,128,128]{2,1,0:T(8,128)(2,1)}, u32[]{:S(2)}, u32[]{:S(2)}) collective-permute-start(bf16[16,128,128]{2,1,0:T(8,128)(2,1)} %slice.169), channel_id=1, source_target_pairs={{0,2},{1,3},{2,0},{3,1},{4,6},{5,7},{6,4},{7,5},{8,10},{9,11},{10,... | collective-permute-start | bytes 1572872 | tf_op jit(solution)/shard_map/ppermute | solution.py:263
  44.1 1.2 collective-permute-start.5
  45.2 4.0 %all-to-all-start.1 = ((bf16[16,64,128]{2,1,0:T(8,128)(2,1)}), bf16[16,64,128]{2,1,0:T(8,128)(2,1)S(1)}, u32[]{:S(2)}, u32[]{:S(2)}) async-start(bf16[16,64,128]{2,1,0:T(8,128)(2,1)} %get-tuple-element.29), calls=%async_computation.1 | async-start | bytes 524288 | tf_op jit(solution)/shard_map/all_to_all | solution.py:271
  49.2 2.6 %collective-permute-start.1 = (bf16[16,96,128]{2,1,0:T(8,128)(2,1)S(1)}, bf16[16,96,128]{2,1,0:T(8,128)(2,1)}, u32[]{:S(2)}, u32[]{:S(2)}) collective-permute-start(bf16[16,96,128]{2,1,0:T(8,128)(2,1)S(1)} %slice.168.refs_0_), channel_id=1, source_target_pairs={{0,16},{4,20},{16,0},{20,4},{1,17},{5,21},{17,1},{21,5},{2,18},{6,... | collective-permute-start | bytes 1179656 | tf_op jit(solution)/shard_map/ppermute | solution.py:263
  51.9 0.0 collective-permute-done.refs_1_
  51.9 1.1 collective-permute-start.2
  52.9 8.0 %all-to-all-done.1 = bf16[16,64,128]{2,1,0:T(8,128)(2,1)S(1)} async-done(((bf16[16,64,128]{2,1,0:T(8,128)(2,1)}), bf16[16,64,128]{2,1,0:T(8,128)(2,1)S(1)}, u32[]{:S(2)}, u32[]{:S(2)}) %all-to-all-start.1) | async-done | bytes 262176 | tf_op jit(solution)/shard_map/all_to_all | solution.py:271
  61.0 1.2 broadcast_in_dim.2
  62.2 0.0 copy-start.3
  62.2 3.6 %all-to-all-start.2 = ((bf16[4,16,64,128]{3,2,1,0:T(8,128)(2,1)}), bf16[4,16,64,128]{3,2,1,0:T(8,128)(2,1)S(1)}, u32[]{:S(2)}, u32[]{:S(2)}) async-start(bf16[4,16,64,128]{3,2,1,0:T(8,128)(2,1)} %broadcast_in_dim.2), calls=%async_computation.2 | async-start | bytes 2097152 | tf_op jit(solution)/shard_map/all_to_all | solution.py:305
  65.9 0.0 collective-permute-done.1.refs_2_
  65.9 0.0 collective-permute-done.3.refs_5_
  65.9 2.2 %collective-permute-done.4.refs_6_ = bf16[16,128,128]{2,1,0:T(8,128)(2,1)} collective-permute-done((bf16[16,128,128]{2,1,0:T(8,128)(2,1)}, bf16[16,128,128]{2,1,0:T(8,128)(2,1)}, u32[]{:S(2)}, u32[]{:S(2)}) %collective-permute-start.4) | collective-permute-done | bytes 524320 | tf_op jit(solution)/shard_map/ppermute | solution.py:263
  68.1 0.0 collective-permute-done.5.refs_7_
  68.1 0.8 collective-permute-done.2.refs_3_
  68.8 0.0 copy-done.3
  68.9 23.5 %attend_own.1 = (bf16[1056,128]{1,0:T(8,128)(2,1)S(1)}, bf16[1056,128]{1,0:T(8,128)(2,1)S(1)}, bf16[1056,128]{1,0:T(8,128)(2,1)S(1)}, bf16[1056,128]{1,0:T(8,128)(2,1)S(1)}) custom-call(s32[4]{0:T(128)S(1)} %copy-done.3, bf16[16,96,128]{2,1,0:T(8,128)(2,1)S(1)} %slice.168.refs_0_, bf16[16,96,128]{2,1,0:T(8,128)(2,1)S(1)} %collective-permute-done.refs_1_, ...), custom_call_target="tpu_custom_call" | custom-call | flops 17179869184 | bytes 4194304 | tf_op jit(solution)/shard_map/attend_own/pallas_call | solution.py:237
  92.4 0.0 copy-start
  92.4 0.7 copy-done
  93.1 0.7 copy-done.1
  93.8 0.7 copy-done.2
  94.5 0.0 all-to-all-done.2.refs_4_
  94.5 1.0 collective-permute-start.9
  95.5 0.0 collective-permute-start.6
  95.5 0.0 collective-permute-start.7
  95.5 1.5 collective-permute-start.8
  97.0 0.8 collective-permute-done.9.refs_5_
  97.8 16.8 %attend_shared.1 = (bf16[528,128]{1,0:T(8,128)(2,1)S(1)}, bf16[528,128]{1,0:T(8,128)(2,1)S(1)}, bf16[528,128]{1,0:T(8,128)(2,1)S(1)}, bf16[528,128]{1,0:T(8,128)(2,1)S(1)}) custom-call(s32[4]{0:T(128)S(1)} %copy-done.3, bf16[16,96,128]{2,1,0:T(8,128)(2,1)S(1)} %slice.168.refs_0_, bf16[16,96,128]{2,1,0:T(8,128)(2,1)S(1)} %collective-permute-done.refs_1_, ...), custom_call_target="tpu_custom_call" | custom-call | flops 8589934592 | bytes 4194304 | tf_op jit(solution)/shard_map/attend_shared/pallas_call | solution.py:237
  114.6 0.0 collective-permute-done.6
  114.6 0.0 collective-permute-done.7
  114.6 0.0 copy-start.4
  114.6 0.0 collective-permute-done.8
  114.6 0.0 copy-start.5
  114.6 0.7 copy-done.4
  115.3 0.1 copy-done.5
  115.4 0.0 slice-start.1
  115.4 0.0 slice-start
  115.5 0.1 collective-permute-start.12
  115.6 0.4 collective-permute-start.11
  116.0 2.3 %collective-permute-start.10 = (bf16[528,128]{1,0:T(8,128)(2,1)S(1)}, bf16[528,128]{1,0:T(8,128)(2,1)S(1)}, u32[]{:S(2)}, u32[]{:S(2)}) collective-permute-start(bf16[528,128]{1,0:T(8,128)(2,1)S(1)} %get-tuple-element.32), channel_id=1, source_target_pairs={{0,20},{4,0},{16,4},{20,16},{1,21},{5,1},{17,5},{21,17},{2,22},{6,... | collective-permute-start | bytes 405512 | tf_op jit(solution)/shard_map/ppermute | solution.py:263
  118.2 0.1 fusion.8
  118.4 0.0 slice-done.1
  118.4 0.0 slice-done
  118.4 0.6 fusion.1
  119.0 5.6 %collective-permute-done.12 = bf16[528,128]{1,0:T(8,128)(2,1)S(1)} collective-permute-done((bf16[528,128]{1,0:T(8,128)(2,1)S(1)}, bf16[528,128]{1,0:T(8,128)(2,1)S(1)}, u32[]{:S(2)}, u32[]{:S(2)}) %collective-permute-start.12) | collective-permute-done | bytes 135200 | tf_op jit(solution)/shard_map/ppermute | solution.py:263
  124.6 0.0 collective-permute-done.11
  124.7 0.1 collective-permute-done.10
  124.8 0.1 fusion.12
  124.9 0.1 mul.87
  125.0 0.1 mul.90
  125.0 0.1 mul.93
  125.1 0.1 mul.84
  125.2 0.1 copy-done.7
  125.3 0.1 copy-done.6
  125.4 0.9 slice-done.2
  126.3 0.1 slice-done.3
  126.4 0.3 fusion.5
  126.8 22.8 %all_to_all.21.ref = bf16[16,96,128]{2,1,0:T(8,128)(2,1)} all-to-all(bf16[16,96,128]{2,1,0:T(8,128)(2,1)S(1)} %pad_maximum_fusion), channel_id=1, replica_groups=mesh['z'=8,'yh'=2,'c'=2,'yl'=2,'x'=4] {'z','c'}, dimensions={0} | all-to-all | bytes 786432 | tf_op jit(solution)/shard_map/all_to_all | solution.py:271
  149.6 1.8 %unpack.1 = bf16[64,3072]{1,0:T(8,128)(2,1)} custom-call(bf16[16,96,128]{2,1,0:T(8,128)(2,1)} %all_to_all.21.ref), custom_call_target="tpu_custom_call" | custom-call | tf_op jit(solution)/shard_map/unpack/pallas_call | solution.py:67
  (20 shorter events, 0.2 us)
Async XLA Ops:
  38.2 13.7 %collective-permute-start = (bf16[16,96,128]{2,1,0:T(8,128)(2,1)S(1)}, bf16[16,96,128]{2,1,0:T(8,128)(2,1)S(1)}, u32[]{:S(2)}, u32[]{:S(2)}) collective-permute-start(bf16[16,96,128]{2,1,0:T(8,128)(2,1)S(1)} %slice.168.refs_0_), channel_id=1, source_target_pairs={{0,4},{4,16},{16,20},{20,0},{1,5},{5,17},{17,21},{21,1},{2,6},{6,1... | collective-permute-start | bytes 1179656 | tf_op jit(solution)/shard_map/ppermute | solution.py:263
  40.4 25.5 %collective-permute-start.3 = (bf16[16,128,128]{2,1,0:T(8,128)(2,1)}, bf16[16,128,128]{2,1,0:T(8,128)(2,1)S(1)}, u32[]{:S(2)}, u32[]{:S(2)}) collective-permute-start(bf16[16,128,128]{2,1,0:T(8,128)(2,1)} %slice.169), channel_id=1, source_target_pairs={{0,1},{1,2},{2,3},{3,0},{4,5},{5,6},{6,7},{7,4},{8,9},{9,10},{10,1... | collective-permute-start | bytes 1572872 | tf_op jit(solution)/shard_map/ppermute | solution.py:263
  41.6 26.5 %collective-permute-start.4 = (bf16[16,128,128]{2,1,0:T(8,128)(2,1)}, bf16[16,128,128]{2,1,0:T(8,128)(2,1)}, u32[]{:S(2)}, u32[]{:S(2)}) collective-permute-start(bf16[16,128,128]{2,1,0:T(8,128)(2,1)} %slice.169), channel_id=1, source_target_pairs={{0,2},{1,3},{2,0},{3,1},{4,6},{5,7},{6,4},{7,5},{8,10},{9,11},{10,... | collective-permute-start | bytes 1572872 | tf_op jit(solution)/shard_map/ppermute | solution.py:263
  44.1 24.0 %collective-permute-start.5 = (bf16[16,128,128]{2,1,0:T(8,128)(2,1)}, bf16[16,128,128]{2,1,0:T(8,128)(2,1)}, u32[]{:S(2)}, u32[]{:S(2)}) collective-permute-start(bf16[16,128,128]{2,1,0:T(8,128)(2,1)} %slice.169), channel_id=1, source_target_pairs={{0,3},{1,0},{2,1},{3,2},{4,7},{5,4},{6,5},{7,6},{8,11},{9,8},{10,9... | collective-permute-start | bytes 1572872 | tf_op jit(solution)/shard_map/ppermute | solution.py:263
  45.2 15.7 %all-to-all-start.1 = ((bf16[16,64,128]{2,1,0:T(8,128)(2,1)}), bf16[16,64,128]{2,1,0:T(8,128)(2,1)S(1)}, u32[]{:S(2)}, u32[]{:S(2)}) async-start(bf16[16,64,128]{2,1,0:T(8,128)(2,1)} %get-tuple-element.29), calls=%async_computation.1 | async-start | bytes 524288 | tf_op jit(solution)/shard_map/all_to_all | solution.py:271
  49.2 16.6 %collective-permute-start.1 = (bf16[16,96,128]{2,1,0:T(8,128)(2,1)S(1)}, bf16[16,96,128]{2,1,0:T(8,128)(2,1)}, u32[]{:S(2)}, u32[]{:S(2)}) collective-permute-start(bf16[16,96,128]{2,1,0:T(8,128)(2,1)S(1)} %slice.168.refs_0_), channel_id=1, source_target_pairs={{0,16},{4,20},{16,0},{20,4},{1,17},{5,21},{17,1},{21,5},{2,18},{6,... | collective-permute-start | bytes 1179656 | tf_op jit(solution)/shard_map/ppermute | solution.py:263
  51.9 17.0 %collective-permute-start.2 = (bf16[16,96,128]{2,1,0:T(8,128)(2,1)S(1)}, bf16[16,96,128]{2,1,0:T(8,128)(2,1)}, u32[]{:S(2)}, u32[]{:S(2)}) collective-permute-start(bf16[16,96,128]{2,1,0:T(8,128)(2,1)S(1)} %slice.168.refs_0_), channel_id=1, source_target_pairs={{0,20},{4,0},{16,4},{20,16},{1,21},{5,1},{17,5},{21,17},{2,22},{6,... | collective-permute-start | bytes 1179656 | tf_op jit(solution)/shard_map/ppermute | solution.py:263
  62.2 6.7 %copy-start.3 = (s32[4]{0:T(128)S(1)}, s32[4]{0:T(128)}, u32[]{:S(2)}) copy-start(s32[4]{0:T(128)} %span_tiles.3) | copy-start | bytes 52
  62.2 32.3 %all-to-all-start.2 = ((bf16[4,16,64,128]{3,2,1,0:T(8,128)(2,1)}), bf16[4,16,64,128]{3,2,1,0:T(8,128)(2,1)S(1)}, u32[]{:S(2)}, u32[]{:S(2)}) async-start(bf16[4,16,64,128]{3,2,1,0:T(8,128)(2,1)} %broadcast_in_dim.2), calls=%async_computation.2 | async-start | bytes 2097152 | tf_op jit(solution)/shard_map/all_to_all | solution.py:305
  92.4 0.7 copy-start
  93.1 0.7 copy-start.1
  93.8 0.7 copy-start.2
  94.5 3.3 %collective-permute-start.9 = (bf16[4,16,64,128]{3,2,1,0:T(8,128)(2,1)S(1)}, bf16[4,16,64,128]{3,2,1,0:T(8,128)(2,1)S(1)}, u32[]{:S(2)}, u32[]{:S(2)}) collective-permute-start(bf16[4,16,64,128]{3,2,1,0:T(8,128)(2,1)S(1)} %all-to-all-done.2.refs_4_), channel_id=1, source_target_pairs={{0,8},{8,0},{1,9},{9,1},{2,10},{10,2},{3,11},{11,3},{4,12},{12,4},... | collective-permute-start | bytes 3145736 | tf_op jit(solution)/shard_map/ppermute | solution.py:309
  95.5 19.0 %collective-permute-start.6 = (bf16[1056,128]{1,0:T(8,128)(2,1)}, bf16[1056,128]{1,0:T(8,128)(2,1)S(1)}, u32[]{:S(2)}, u32[]{:S(2)}) collective-permute-start(bf16[1056,128]{1,0:T(8,128)(2,1)} %copy-done.2), channel_id=1, source_target_pairs={{0,20},{4,0},{16,4},{20,16},{1,21},{5,1},{17,5},{21,17},{2,22},{6,... | collective-permute-start | bytes 811016 | tf_op jit(solution)/shard_map/ppermute | solution.py:263
  95.5 19.1 %collective-permute-start.7 = (bf16[1056,128]{1,0:T(8,128)(2,1)}, bf16[1056,128]{1,0:T(8,128)(2,1)S(1)}, u32[]{:S(2)}, u32[]{:S(2)}) collective-permute-start(bf16[1056,128]{1,0:T(8,128)(2,1)} %copy-done.1), channel_id=1, source_target_pairs={{0,16},{4,20},{16,0},{20,4},{1,17},{5,21},{17,1},{21,5},{2,18},{6,... | collective-permute-start | bytes 811016 | tf_op jit(solution)/shard_map/ppermute | solution.py:263
  95.5 19.1 %collective-permute-start.8 = (bf16[1056,128]{1,0:T(8,128)(2,1)}, bf16[1056,128]{1,0:T(8,128)(2,1)S(1)}, u32[]{:S(2)}, u32[]{:S(2)}) collective-permute-start(bf16[1056,128]{1,0:T(8,128)(2,1)} %copy-done), channel_id=1, source_target_pairs={{0,4},{4,16},{16,20},{20,0},{1,5},{5,17},{17,21},{21,1},{2,6},{6,1... | collective-permute-start | bytes 811016 | tf_op jit(solution)/shard_map/ppermute | solution.py:263
  114.6 0.7 copy-start.4
  114.6 0.8 copy-start.5
  115.4 2.9 %slice-start.1 = ((bf16[1056,128]{1,0:T(8,128)(2,1)}), bf16[1024,128]{1,0:T(8,128)(2,1)S(1)}, s32[]{:S(2)}) async-start(bf16[1056,128]{1,0:T(8,128)(2,1)} %copy-done.5), calls=%async_computation.5 | async-start | bytes 524288 | tf_op jit(solution)/shard_map/slice | solution.py:285
  115.4 2.9 %slice-start = ((bf16[1056,128]{1,0:T(8,128)(2,1)}), bf16[1024,128]{1,0:T(8,128)(2,1)S(1)}, s32[]{:S(2)}) async-start(bf16[1056,128]{1,0:T(8,128)(2,1)} %copy-done.4), calls=%async_computation.4 | async-start | bytes 524288 | tf_op jit(solution)/shard_map/slice | solution.py:285
  115.5 9.2 %collective-permute-start.12 = (bf16[528,128]{1,0:T(8,128)(2,1)S(1)}, bf16[528,128]{1,0:T(8,128)(2,1)S(1)}, u32[]{:S(2)}, u32[]{:S(2)}) collective-permute-start(bf16[528,128]{1,0:T(8,128)(2,1)S(1)} %get-tuple-element.34), channel_id=1, source_target_pairs={{0,4},{4,16},{16,20},{20,0},{1,5},{5,17},{17,21},{21,1},{2,6},{6,1... | collective-permute-start | bytes 405512 | tf_op jit(solution)/shard_map/ppermute | solution.py:263
  115.6 9.1 %collective-permute-start.11 = (bf16[528,128]{1,0:T(8,128)(2,1)S(1)}, bf16[528,128]{1,0:T(8,128)(2,1)S(1)}, u32[]{:S(2)}, u32[]{:S(2)}) collective-permute-start(bf16[528,128]{1,0:T(8,128)(2,1)S(1)} %get-tuple-element.33), channel_id=1, source_target_pairs={{0,16},{4,20},{16,0},{20,4},{1,17},{5,21},{17,1},{21,5},{2,18},{6,... | collective-permute-start | bytes 405512 | tf_op jit(solution)/shard_map/ppermute | solution.py:263
  116.0 8.8 %collective-permute-start.10 = (bf16[528,128]{1,0:T(8,128)(2,1)S(1)}, bf16[528,128]{1,0:T(8,128)(2,1)S(1)}, u32[]{:S(2)}, u32[]{:S(2)}) collective-permute-start(bf16[528,128]{1,0:T(8,128)(2,1)S(1)} %get-tuple-element.32), channel_id=1, source_target_pairs={{0,20},{4,0},{16,4},{20,16},{1,21},{5,1},{17,5},{21,17},{2,22},{6,... | collective-permute-start | bytes 405512 | tf_op jit(solution)/shard_map/ppermute | solution.py:263
  124.6 0.7 copy-start.7
  124.8 0.6 copy-start.6
  125.4 0.9 slice-start.2
  125.4 1.0 slice-start.3
where the time goes:
time: 150 us; the launch traced here: 151 us
  blocking collectives  58.5 us (39%)
  Pallas kernels  44.5 us (30%)
  starting transfers between devices  22.8 us (15%)
  waiting for transfers between devices  17.6 us (12%)
  local copies, waits for them, and re-layouts  6.55 us (4%)
    all_to_all x2, blocking collectives, along_z(): lax.all_to_all(array, ('z', 'c'), split_axis=0, concat_axis=0, tiled=True)  58.5 us
    pallas_call x2, Pallas kernels, attend(): pl.pallas_call(functools.partial(attend_kernel, shared, planes, join), in...  40.3 us
    ppermute x12, starting transfers between devices, turn(): lax.ppermute(array, axis, [(i, (i + by) % size) for i in range(size)])  14.1 us
    ppermute x12, waiting for transfers between devices, turn(): lax.ppermute(array, axis, [(i, (i + by) % size) for i in range(size)])  8.73 us
    all_to_all x1, waiting for transfers between devices, along_z(): lax.all_to_all(array, ('z', 'c'), split_axis=0, concat_axis=0, tiled=True)  8.01 us
    all_to_all x1, starting transfers between devices, along_z(): lax.all_to_all(array, ('z', 'c'), split_axis=0, concat_axis=0, tiled=True)  4 us
    all_to_all x1, starting transfers between devices, body(): lax.all_to_all(jnp.broadcast_to(rest, (X, *rest.shape)), 'x', split_axis=...  3.65 us
    unnamed x16, local copies, waits for them, and re-layouts  3.14 us
  transfers between devices with their start and end apart: 15, of which 6 were waited for; matrix products, arithmetic and copies ran while one was open for 2% of the time, Pallas kernels for 27%

commit v1 on v0

--- a/solution.py
+++ b/solution.py
@@ -17,6 +17,7 @@
 HEADS_HERE = 3
 QT = Y * TOK
 KT = X * TOK
+PLANES = 4
 CHUNKS = Z * CORES
 GROUP = 4
 VROWS = HD + 16
@@ -27,7 +28,7 @@
 
 
 def pack_kernel(q_ref, k_ref, v_ref, most, rest):
-    for plane in range(Z):
+    for plane in range(PLANES):
         for core in range(CORES):
             to = plane * CORES + core
             half = slice(core * HALF, (core + 1) * HALF)
@@ -43,8 +44,12 @@
 
 
 def pack(queries, keys, values):
+    blocks = [(PLANES * CORES, 3 * TOK + HALF, HD), (PLANES * CORES, TOK, HD)]
     return pl.pallas_call(
         pack_kernel,
+        grid=(Z // PLANES,),
+        in_specs=[pl.BlockSpec((TOK, PLANES * HEADS_HERE * HD), lambda i: (0, i))] * 3,
+        out_specs=[pl.BlockSpec(block, lambda i: (i, 0, 0)) for block in blocks],
         out_shape=[
             jax.ShapeDtypeStruct((CHUNKS, 3 * TOK + HALF, HD), jnp.bfloat16),
             jax.ShapeDtypeStruct((CHUNKS, TOK, HD), jnp.bfloat16),
@@ -54,7 +59,7 @@
 
 
 def unpack_kernel(ref, out):
-    for plane in range(Z):
+    for plane in range(PLANES):
         for core in range(CORES):
             at = plane * CORES + core
             lo = (plane * HEADS_HERE + 1 + core) * HD
@@ -66,6 +71,9 @@
 def unpack(parts):
     return pl.pallas_call(
         unpack_kernel,
+        grid=(Z // PLANES,),
+        in_specs=[pl.BlockSpec((PLANES * CORES, TOK + HALF, HD), lambda i: (i, 0, 0))],
+        out_specs=pl.BlockSpec((TOK, PLANES * HEADS_HERE * HD), lambda i: (0, i)),
         out_shape=jax.ShapeDtypeStruct((TOK, Z * HEADS_HERE * HD), jnp.bfloat16),
         name="unpack",
     )(parts)
@@ -75,7 +83,7 @@
     qs, refs = refs[:Y], refs[Y:]
     mine, refs = (refs[:CORES], refs[CORES:]) if shared else (refs[:X], refs[X:])
     o_refs, refs = refs[:Y], refs[Y:]
-    k_scr, v_scr, s_scr, q_scr, limit_scr, acc_scr, top_scr, steps, q_in, v_in, o_scr, sems = refs
+    k_scr, v_scr, s_scr, q_scr, limit_scr, acc_scr, top_scr, steps, q_in, v_in, sems = refs
     x = lax.axis_index("x")
     y = lax.axis_index("yh") * YL + lax.axis_index("yl")
     bounds = [span_tiles[0] * TILE]
@@ -111,9 +119,10 @@
     def chunk_start(j):
         return (j // CORES) * (TOK * 32) + (j % CORES) * (TOK * 8) + y_off
 
-    def arrange_values(j, carry):
-        v_scr[j, 0:HD, :] = v_in[j].T
-        v_scr[j, HD:VROWS, :] = ones
+    def arrange_values(m, carry):
+        for g in range(GROUP):
+            v_scr[m, 0:HD, g * KT:(g + 1) * KT] = v_in[m * GROUP + g].T
+            v_scr[m, HD:VROWS, g * KT:(g + 1) * KT] = ones
         return carry
 
     def arrange_queries(t, whole):
@@ -130,8 +139,8 @@
             high = q.astype(jnp.bfloat16)
             low = (q - high.astype(jnp.float32)).astype(jnp.bfloat16)
             at = slice(part * QT, (part + 1) * QT)
-            q_scr[t, at, 0:HD] = high
-            q_scr[t, at, HD:2 * HD] = low
+            q_scr[t, 0:HD, at] = high.T
+            q_scr[t, HD:2 * HD, at] = low.T
             row = jnp.zeros((1, QT), jnp.int32)
             for block in range(QT // size):
                 yq = (y + Y - (block * size) // TOK) % Y
@@ -156,7 +165,7 @@
     rounds = lax.fori_loop(0, tiles, arrange_queries, jnp.int32(0))
     for copy in copies[1]:
         copy.wait()
-    lax.fori_loop(0, CHUNKS, arrange_values, 0)
+    lax.fori_loop(0, CHUNKS // GROUP, arrange_values, 0)
     for copy in copies[2]:
         copy.wait()
 
@@ -166,7 +175,7 @@
         return [jnp.where(start + ((x + X - d) % X) * TOK < limit_row, 0.0, LOW) for d in range(X)]
 
     def produce(t, j, slot, best):
-        s = lax.dot_general(k_scr[j], q_scr[t], (((1,), (1,)), ((), ())), preferred_element_type=jnp.float32)
+        s = jnp.dot(k_scr[j], q_scr[t], preferred_element_type=jnp.float32)
         s_scr[slot] = s
         for d, bias in enumerate(bias_rows(t, j)):
             part = jnp.max(s[d * TOK:(d + 1) * TOK].reshape(TOK // 8, 8, wide), axis=0) + bias
@@ -188,12 +197,13 @@
         n2 = jnp.where(last, 0, n + 1)
         best = jnp.where(last, FLOOR, best)
         accum = acc_scr[t] * jnp.exp2(old - top)
+        ps = []
         for g in range(GROUP):
             j = n * GROUP + g
             p = consume(t, j, g, top)
             best = produce(t2, n2 * GROUP + g, g, best)
-            accum = accum + jnp.dot(v_scr[j], p, preferred_element_type=jnp.float32)
-        acc_scr[t] = accum
+            ps.append(p)
+        acc_scr[t] = accum + jnp.dot(v_scr[n], jnp.concatenate(ps, axis=0), preferred_element_type=jnp.float32)
         top_scr[t, 0:1, :] = top
         return t2, n2, best, jnp.where(last, FLOOR, top)
 
@@ -210,7 +220,7 @@
         stats.append(jnp.where(some, top_scr[t, 0:1, at] + jnp.log2(safe), LOW))
         out = (acc_scr[t, 0:HD, at] * (1.0 / safe)).T.astype(jnp.bfloat16)
         for d in range(Y):
-            o_scr[d, i * TOK:(i + 1) * TOK, :] = out[d * TOK:(d + 1) * TOK]
+            o_refs[d][i * TOK:(i + 1) * TOK, :] = out[d * TOK:(d + 1) * TOK]
     lse = jnp.concatenate(stats, axis=0)
     high = lse.astype(jnp.bfloat16)
     lse = lse - high.astype(jnp.float32)
@@ -220,12 +230,7 @@
         at = slice(d * TOK, (d + 1) * TOK)
         first = jnp.concatenate([high[:, at], middle[:, at]], axis=1)
         second = jnp.concatenate([low[:, at], jnp.zeros((planes, HD - TOK), jnp.bfloat16)], axis=1)
-        o_scr[d, rows:rows + 2 * planes, :] = jnp.concatenate([first, second], axis=0)
-    out_copies = [pltpu.make_async_copy(o_scr.at[d], o_refs[d], sems.at[d]) for d in range(Y)]
-    for copy in out_copies:
-        copy.start()
-    for copy in out_copies:
-        copy.wait()
+        o_refs[d][rows:rows + 2 * planes, :] = jnp.concatenate([first, second], axis=0)
 
 
 def attend(span_tiles, shared, qs, mine):
@@ -237,23 +242,22 @@
     return pl.pallas_call(
         functools.partial(attend_kernel, shared, planes, join),
         in_specs=[pl.BlockSpec(memory_space=pltpu.SMEM)] + [pl.BlockSpec(memory_space=pl.ANY)] * len(arrays),
-        out_specs=[pl.BlockSpec(memory_space=pl.ANY)] * Y,
-        out_shape=[jax.ShapeDtypeStruct((planes * (TOK + 2), HD), jnp.bfloat16)] * Y,
+        out_specs=[pl.BlockSpec(memory_space=pltpu.VMEM)] * Y,
+        out_shape=[pltpu.VMEM((planes * (TOK + 2), HD), jnp.bfloat16)] * Y,
         scratch_shapes=[
             pltpu.VMEM((CHUNKS, KT, 2 * HD), jnp.bfloat16),
-            pltpu.VMEM((CHUNKS, VROWS, KT), jnp.bfloat16),
+            pltpu.VMEM((CHUNKS // GROUP, VROWS, GROUP * KT), jnp.bfloat16),
             pltpu.VMEM((GROUP, KT, wide), jnp.float32),
-            pltpu.VMEM((tiles, wide, 2 * HD), jnp.bfloat16),
+            pltpu.VMEM((tiles, 2 * HD, wide), jnp.bfloat16),
             pltpu.VMEM((tiles, 8, wide), jnp.int32),
             pltpu.VMEM((tiles, VROWS, wide), jnp.float32),
             pltpu.VMEM((tiles, 8, wide), jnp.float32),
             pltpu.SMEM((tiles,), jnp.int32),
             pltpu.VMEM((Y, CHUNKS, HALF if shared else TOK, HD), jnp.bfloat16),
             pltpu.VMEM((CHUNKS, KT, HD), jnp.bfloat16),
-            pltpu.VMEM((Y, planes * (TOK + 2), HD), jnp.bfloat16),
             pltpu.SemaphoreType.DMA((Y + 3 * X * (2 if shared else 1),)),
         ],
-        compiler_params=pltpu.CompilerParams(vmem_limit_bytes=30 * 1024 * 1024),
+        compiler_params=pltpu.CompilerParams(vmem_limit_bytes=(20 if shared else 28) * 1024 * 1024),
         cost_estimate=pl.CostEstimate(flops=8 * pairs * HD, bytes_accessed=4 << 20, transcendentals=pairs),
         name="attend_shared" if shared else "attend_own",
     )(span_tiles, *arrays)

time: 150 us -> 146 us (0.973)
  Pallas kernels: 44.5 us -> 39.1 us
    pallas_call x2, Pallas kernels: 40.3 us -> 35.1 us  [attend(): pl.pallas_call(functools.partial(attend_kernel, shared, planes, join), in...]
  transfers between devices with their start and end apart: 15 -> 15, of which waited for: 6 -> 6; matrix products, arithmetic and copies ran while one was open for 2% -> 2% of each run, Pallas kernels for 27% -> 24%
where the time goes in v1:
time: 146 us
  blocking collectives  58.6 us (40%)
  Pallas kernels  39.1 us (27%)
  starting transfers between devices  23.5 us (16%)
  waiting for transfers between devices  16.8 us (12%)
  local copies, waits for them, and re-layouts  6.55 us (4%)
    all_to_all x2, blocking collectives, along_z(): lax.all_to_all(array, ('z', 'c'), split_axis=0, concat_axis=0, tiled=True)  58.6 us
    pallas_call x2, Pallas kernels, attend(): pl.pallas_call(functools.partial(attend_kernel, shared, planes, join), in...  35.1 us
    ppermute x12, starting transfers between devices, turn(): lax.ppermute(array, axis, [(i, (i + by) % size) for i in range(size)])  14.9 us
    all_to_all x1, waiting for transfers between devices, along_z(): lax.all_to_all(array, ('z', 'c'), split_axis=0, concat_axis=0, tiled=True)  8.01 us
    ppermute x12, waiting for transfers between devices, turn(): lax.ppermute(array, axis, [(i, (i + by) % size) for i in range(size)])  7.92 us
    all_to_all x1, starting transfers between devices, along_z(): lax.all_to_all(array, ('z', 'c'), split_axis=0, concat_axis=0, tiled=True)  4 us
    all_to_all x1, starting transfers between devices, body(): lax.all_to_all(jnp.broadcast_to(rest, (X, *rest.shape)), 'x', split_axis=...  3.65 us
    unnamed x16, local copies, waits for them, and re-layouts  3.14 us
  transfers between devices with their start and end apart: 15, of which 6 were waited for; matrix products, arithmetic and copies ran while one was open for 2% of the time, Pallas kernels for 24%

profile of v1, /device:TPU:1, one launch (start us, length us, event | category | flops | bytes accessed | tf_op | source)
XLA Modules:
  0.0 146.0 jit_solution(2667468663757292365)
XLA Ops:
  0.0 2.3 %pack.1 = (bf16[16,224,128]{2,1,0:T(8,128)(2,1)}, bf16[16,64,128]{2,1,0:T(8,128)(2,1)}) custom-call(bf16[64,3072]{1,0:T(8,128)(2,1)} %q_ref.1, bf16[64,3072]{1,0:T(8,128)(2,1)} %k_ref.1, bf16[64,3072]{1,0:T(8,128)(2,1)} %v_ref.1), custom_call_target="tpu_custom_call" | custom-call | tf_op jit(solution)/shard_map/pack/pallas_call | solution.py:48
  2.3 35.7 %all_to_all.20.refs_4_ = bf16[16,224,128]{2,1,0:T(8,128)(2,1)S(1)} all-to-all(bf16[16,224,128]{2,1,0:T(8,128)(2,1)} %get-tuple-element.22), channel_id=1, replica_groups=mesh['z'=8,'yh'=2,'c'=2,'yl'=2,'x'=4] {'z','c'}, dimensions={0} | all-to-all | bytes 1835008 | tf_op jit(solution)/shard_map/all_to_all | solution.py:275
  38.0 1.4 collective-permute-start
  39.4 0.8 slice.169
  40.2 1.2 collective-permute-start.3
  41.4 2.5 %collective-permute-start.4 = (bf16[16,128,128]{2,1,0:T(8,128)(2,1)}, bf16[16,128,128]{2,1,0:T(8,128)(2,1)}, u32[]{:S(2)}, u32[]{:S(2)}) collective-permute-start(bf16[16,128,128]{2,1,0:T(8,128)(2,1)} %slice.169), channel_id=1, source_target_pairs={{0,2},{1,3},{2,0},{3,1},{4,6},{5,7},{6,4},{7,5},{8,10},{9,11},{10,... | collective-permute-start | bytes 1572872 | tf_op jit(solution)/shard_map/ppermute | solution.py:267
  43.9 1.2 collective-permute-start.5
  45.1 4.0 %all-to-all-start.1 = ((bf16[16,64,128]{2,1,0:T(8,128)(2,1)}), bf16[16,64,128]{2,1,0:T(8,128)(2,1)S(1)}, u32[]{:S(2)}, u32[]{:S(2)}) async-start(bf16[16,64,128]{2,1,0:T(8,128)(2,1)} %get-tuple-element.29), calls=%async_computation.1 | async-start | bytes 524288 | tf_op jit(solution)/shard_map/all_to_all | solution.py:275
  49.1 2.6 %collective-permute-start.1 = (bf16[16,96,128]{2,1,0:T(8,128)(2,1)S(1)}, bf16[16,96,128]{2,1,0:T(8,128)(2,1)}, u32[]{:S(2)}, u32[]{:S(2)}) collective-permute-start(bf16[16,96,128]{2,1,0:T(8,128)(2,1)S(1)} %slice.168.refs_0_), channel_id=1, source_target_pairs={{0,16},{4,20},{16,0},{20,4},{1,17},{5,21},{17,1},{21,5},{2,18},{6,... | collective-permute-start | bytes 1179656 | tf_op jit(solution)/shard_map/ppermute | solution.py:267
  51.7 0.0 collective-permute-done.refs_1_
  51.7 1.1 collective-permute-start.2
  52.8 8.0 %all-to-all-done.1 = bf16[16,64,128]{2,1,0:T(8,128)(2,1)S(1)} async-done(((bf16[16,64,128]{2,1,0:T(8,128)(2,1)}), bf16[16,64,128]{2,1,0:T(8,128)(2,1)S(1)}, u32[]{:S(2)}, u32[]{:S(2)}) %all-to-all-start.1) | async-done | bytes 262176 | tf_op jit(solution)/shard_map/all_to_all | solution.py:275
  60.8 1.2 broadcast_in_dim.2
  62.0 0.0 copy-start.3
  62.0 3.6 %all-to-all-start.2 = ((bf16[4,16,64,128]{3,2,1,0:T(8,128)(2,1)}), bf16[4,16,64,128]{3,2,1,0:T(8,128)(2,1)S(1)}, u32[]{:S(2)}, u32[]{:S(2)}) async-start(bf16[4,16,64,128]{3,2,1,0:T(8,128)(2,1)} %broadcast_in_dim.2), calls=%async_computation.2 | async-start | bytes 2097152 | tf_op jit(solution)/shard_map/all_to_all | solution.py:309
  65.7 0.0 collective-permute-done.1.refs_2_
  65.7 0.0 collective-permute-done.3.refs_5_
  65.7 2.2 %collective-permute-done.4.refs_6_ = bf16[16,128,128]{2,1,0:T(8,128)(2,1)} collective-permute-done((bf16[16,128,128]{2,1,0:T(8,128)(2,1)}, bf16[16,128,128]{2,1,0:T(8,128)(2,1)}, u32[]{:S(2)}, u32[]{:S(2)}) %collective-permute-start.4) | collective-permute-done | bytes 524320 | tf_op jit(solution)/shard_map/ppermute | solution.py:267
  67.9 0.0 collective-permute-done.5.refs_7_
  67.9 0.8 collective-permute-done.2.refs_3_
  68.7 0.0 copy-done.3
  68.7 21.5 %attend_own.1 = (bf16[1056,128]{1,0:T(8,128)(2,1)S(1)}, bf16[1056,128]{1,0:T(8,128)(2,1)S(1)}, bf16[1056,128]{1,0:T(8,128)(2,1)S(1)}, bf16[1056,128]{1,0:T(8,128)(2,1)S(1)}) custom-call(s32[4]{0:T(128)S(1)} %copy-done.3, bf16[16,96,128]{2,1,0:T(8,128)(2,1)S(1)} %slice.168.refs_0_, bf16[16,96,128]{2,1,0:T(8,128)(2,1)S(1)} %collective-permute-done.refs_1_, ...), custom_call_target="tpu_custom_call" | custom-call | flops 17179869184 | bytes 4194304 | tf_op jit(solution)/shard_map/attend_own/pallas_call | solution.py:242
  90.1 0.0 copy-start
  90.1 0.7 copy-done
  90.8 0.7 copy-done.1
  91.6 0.7 copy-done.2
  92.3 0.0 all-to-all-done.2.refs_4_
  92.3 1.0 collective-permute-start.9
  93.3 0.0 collective-permute-start.6
  93.3 0.8 collective-permute-start.7
  94.0 0.7 collective-permute-start.8
  94.7 0.8 collective-permute-done.9.refs_5_
  95.6 13.7 %attend_shared.1 = (bf16[528,128]{1,0:T(8,128)(2,1)S(1)}, bf16[528,128]{1,0:T(8,128)(2,1)S(1)}, bf16[528,128]{1,0:T(8,128)(2,1)S(1)}, bf16[528,128]{1,0:T(8,128)(2,1)S(1)}) custom-call(s32[4]{0:T(128)S(1)} %copy-done.3, bf16[16,96,128]{2,1,0:T(8,128)(2,1)S(1)} %slice.168.refs_0_, bf16[16,96,128]{2,1,0:T(8,128)(2,1)S(1)} %collective-permute-done.refs_1_, ...), custom_call_target="tpu_custom_call" | custom-call | flops 8589934592 | bytes 4194304 | tf_op jit(solution)/shard_map/attend_shared/pallas_call | solution.py:242
  109.3 0.0 collective-permute-done.6
  109.3 0.0 collective-permute-done.7
  109.3 0.0 copy-start.4
  109.3 0.0 collective-permute-done.8
  109.3 0.0 copy-start.5
  109.3 0.7 copy-done.4
  110.0 0.1 copy-done.5
  110.1 0.0 slice-start.1
  110.1 0.0 slice-start
  110.2 0.1 collective-permute-start.12
  110.2 1.7 %collective-permute-start.11 = (bf16[528,128]{1,0:T(8,128)(2,1)S(1)}, bf16[528,128]{1,0:T(8,128)(2,1)S(1)}, u32[]{:S(2)}, u32[]{:S(2)}) collective-permute-start(bf16[528,128]{1,0:T(8,128)(2,1)S(1)} %get-tuple-element.33), channel_id=1, source_target_pairs={{0,16},{4,20},{16,0},{20,4},{1,17},{5,21},{17,1},{21,5},{2,18},{6,... | collective-permute-start | bytes 405512 | tf_op jit(solution)/shard_map/ppermute | solution.py:267
  111.9 1.7 %collective-permute-start.10 = (bf16[528,128]{1,0:T(8,128)(2,1)S(1)}, bf16[528,128]{1,0:T(8,128)(2,1)S(1)}, u32[]{:S(2)}, u32[]{:S(2)}) collective-permute-start(bf16[528,128]{1,0:T(8,128)(2,1)S(1)} %get-tuple-element.32), channel_id=1, source_target_pairs={{0,20},{4,0},{16,4},{20,16},{1,21},{5,1},{17,5},{21,17},{2,22},{6,... | collective-permute-start | bytes 405512 | tf_op jit(solution)/shard_map/ppermute | solution.py:267
  113.7 0.1 fusion.8
  113.8 0.0 slice-done.1
  113.8 0.0 slice-done
  113.8 0.6 fusion.1
  114.5 4.8 %collective-permute-done.12 = bf16[528,128]{1,0:T(8,128)(2,1)S(1)} collective-permute-done((bf16[528,128]{1,0:T(8,128)(2,1)S(1)}, bf16[528,128]{1,0:T(8,128)(2,1)S(1)}, u32[]{:S(2)}, u32[]{:S(2)}) %collective-permute-start.12) | collective-permute-done | bytes 135200 | tf_op jit(solution)/shard_map/ppermute | solution.py:267
  119.2 0.0 collective-permute-done.11
  119.3 0.1 collective-permute-done.10
  119.4 0.1 fusion.12
  119.5 0.1 mul.87
  119.6 0.1 mul.90
  119.7 0.1 mul.93
  119.7 0.1 mul.84
  119.8 0.1 copy-done.7
  119.9 0.1 copy-done.6
  120.1 0.9 slice-done.2
  121.0 0.1 slice-done.3
  121.0 0.3 fusion.5
  121.4 22.8 %all_to_all.21.ref = bf16[16,96,128]{2,1,0:T(8,128)(2,1)} all-to-all(bf16[16,96,128]{2,1,0:T(8,128)(2,1)S(1)} %pad_maximum_fusion), channel_id=1, replica_groups=mesh['z'=8,'yh'=2,'c'=2,'yl'=2,'x'=4] {'z','c'}, dimensions={0} | all-to-all | bytes 786432 | tf_op jit(solution)/shard_map/all_to_all | solution.py:275
  144.2 1.7 %unpack.1 = bf16[64,3072]{1,0:T(8,128)(2,1)} custom-call(bf16[16,96,128]{2,1,0:T(8,128)(2,1)} %all_to_all.21.ref), custom_call_target="tpu_custom_call" | custom-call | tf_op jit(solution)/shard_map/unpack/pallas_call | solution.py:72
  (20 shorter events, 0.2 us)
Async XLA Ops:
  38.0 13.7 %collective-permute-start = (bf16[16,96,128]{2,1,0:T(8,128)(2,1)S(1)}, bf16[16,96,128]{2,1,0:T(8,128)(2,1)S(1)}, u32[]{:S(2)}, u32[]{:S(2)}) collective-permute-start(bf16[16,96,128]{2,1,0:T(8,128)(2,1)S(1)} %slice.168.refs_0_), channel_id=1, source_target_pairs={{0,4},{4,16},{16,20},{20,0},{1,5},{5,17},{17,21},{21,1},{2,6},{6,1... | collective-permute-start | bytes 1179656 | tf_op jit(solution)/shard_map/ppermute | solution.py:267
  40.2 25.5 %collective-permute-start.3 = (bf16[16,128,128]{2,1,0:T(8,128)(2,1)}, bf16[16,128,128]{2,1,0:T(8,128)(2,1)S(1)}, u32[]{:S(2)}, u32[]{:S(2)}) collective-permute-start(bf16[16,128,128]{2,1,0:T(8,128)(2,1)} %slice.169), channel_id=1, source_target_pairs={{0,1},{1,2},{2,3},{3,0},{4,5},{5,6},{6,7},{7,4},{8,9},{9,10},{10,1... | collective-permute-start | bytes 1572872 | tf_op jit(solution)/shard_map/ppermute | solution.py:267
  41.4 26.5 %collective-permute-start.4 = (bf16[16,128,128]{2,1,0:T(8,128)(2,1)}, bf16[16,128,128]{2,1,0:T(8,128)(2,1)}, u32[]{:S(2)}, u32[]{:S(2)}) collective-permute-start(bf16[16,128,128]{2,1,0:T(8,128)(2,1)} %slice.169), channel_id=1, source_target_pairs={{0,2},{1,3},{2,0},{3,1},{4,6},{5,7},{6,4},{7,5},{8,10},{9,11},{10,... | collective-permute-start | bytes 1572872 | tf_op jit(solution)/shard_map/ppermute | solution.py:267
  43.9 24.0 %collective-permute-start.5 = (bf16[16,128,128]{2,1,0:T(8,128)(2,1)}, bf16[16,128,128]{2,1,0:T(8,128)(2,1)}, u32[]{:S(2)}, u32[]{:S(2)}) collective-permute-start(bf16[16,128,128]{2,1,0:T(8,128)(2,1)} %slice.169), channel_id=1, source_target_pairs={{0,3},{1,0},{2,1},{3,2},{4,7},{5,4},{6,5},{7,6},{8,11},{9,8},{10,9... | collective-permute-start | bytes 1572872 | tf_op jit(solution)/shard_map/ppermute | solution.py:267
  45.1 15.7 %all-to-all-start.1 = ((bf16[16,64,128]{2,1,0:T(8,128)(2,1)}), bf16[16,64,128]{2,1,0:T(8,128)(2,1)S(1)}, u32[]{:S(2)}, u32[]{:S(2)}) async-start(bf16[16,64,128]{2,1,0:T(8,128)(2,1)} %get-tuple-element.29), calls=%async_computation.1 | async-start | bytes 524288 | tf_op jit(solution)/shard_map/all_to_all | solution.py:275
  49.1 16.6 %collective-permute-start.1 = (bf16[16,96,128]{2,1,0:T(8,128)(2,1)S(1)}, bf16[16,96,128]{2,1,0:T(8,128)(2,1)}, u32[]{:S(2)}, u32[]{:S(2)}) collective-permute-start(bf16[16,96,128]{2,1,0:T(8,128)(2,1)S(1)} %slice.168.refs_0_), channel_id=1, source_target_pairs={{0,16},{4,20},{16,0},{20,4},{1,17},{5,21},{17,1},{21,5},{2,18},{6,... | collective-permute-start | bytes 1179656 | tf_op jit(solution)/shard_map/ppermute | solution.py:267
  51.7 17.0 %collective-permute-start.2 = (bf16[16,96,128]{2,1,0:T(8,128)(2,1)S(1)}, bf16[16,96,128]{2,1,0:T(8,128)(2,1)}, u32[]{:S(2)}, u32[]{:S(2)}) collective-permute-start(bf16[16,96,128]{2,1,0:T(8,128)(2,1)S(1)} %slice.168.refs_0_), channel_id=1, source_target_pairs={{0,20},{4,0},{16,4},{20,16},{1,21},{5,1},{17,5},{21,17},{2,22},{6,... | collective-permute-start | bytes 1179656 | tf_op jit(solution)/shard_map/ppermute | solution.py:267
  62.0 6.7 %copy-start.3 = (s32[4]{0:T(128)S(1)}, s32[4]{0:T(128)}, u32[]{:S(2)}) copy-start(s32[4]{0:T(128)} %span_tiles.3) | copy-start | bytes 52
  62.0 30.3 %all-to-all-start.2 = ((bf16[4,16,64,128]{3,2,1,0:T(8,128)(2,1)}), bf16[4,16,64,128]{3,2,1,0:T(8,128)(2,1)S(1)}, u32[]{:S(2)}, u32[]{:S(2)}) async-start(bf16[4,16,64,128]{3,2,1,0:T(8,128)(2,1)} %broadcast_in_dim.2), calls=%async_computation.2 | async-start | bytes 2097152 | tf_op jit(solution)/shard_map/all_to_all | solution.py:309
  90.1 0.7 copy-start
  90.8 0.7 copy-start.1
  91.6 0.7 copy-start.2
  92.3 3.3 %collective-permute-start.9 = (bf16[4,16,64,128]{3,2,1,0:T(8,128)(2,1)S(1)}, bf16[4,16,64,128]{3,2,1,0:T(8,128)(2,1)S(1)}, u32[]{:S(2)}, u32[]{:S(2)}) collective-permute-start(bf16[4,16,64,128]{3,2,1,0:T(8,128)(2,1)S(1)} %all-to-all-done.2.refs_4_), channel_id=1, source_target_pairs={{0,8},{8,0},{1,9},{9,1},{2,10},{10,2},{3,11},{11,3},{4,12},{12,4},... | collective-permute-start | bytes 3145736 | tf_op jit(solution)/shard_map/ppermute | solution.py:313
  93.3 16.0 %collective-permute-start.6 = (bf16[1056,128]{1,0:T(8,128)(2,1)}, bf16[1056,128]{1,0:T(8,128)(2,1)S(1)}, u32[]{:S(2)}, u32[]{:S(2)}) collective-permute-start(bf16[1056,128]{1,0:T(8,128)(2,1)} %copy-done.2), channel_id=1, source_target_pairs={{0,20},{4,0},{16,4},{20,16},{1,21},{5,1},{17,5},{21,17},{2,22},{6,... | collective-permute-start | bytes 811016 | tf_op jit(solution)/shard_map/ppermute | solution.py:267
  93.3 16.0 %collective-permute-start.7 = (bf16[1056,128]{1,0:T(8,128)(2,1)}, bf16[1056,128]{1,0:T(8,128)(2,1)S(1)}, u32[]{:S(2)}, u32[]{:S(2)}) collective-permute-start(bf16[1056,128]{1,0:T(8,128)(2,1)} %copy-done.1), channel_id=1, source_target_pairs={{0,16},{4,20},{16,0},{20,4},{1,17},{5,21},{17,1},{21,5},{2,18},{6,... | collective-permute-start | bytes 811016 | tf_op jit(solution)/shard_map/ppermute | solution.py:267
  94.0 15.3 %collective-permute-start.8 = (bf16[1056,128]{1,0:T(8,128)(2,1)}, bf16[1056,128]{1,0:T(8,128)(2,1)S(1)}, u32[]{:S(2)}, u32[]{:S(2)}) collective-permute-start(bf16[1056,128]{1,0:T(8,128)(2,1)} %copy-done), channel_id=1, source_target_pairs={{0,4},{4,16},{16,20},{20,0},{1,5},{5,17},{17,21},{21,1},{2,6},{6,1... | collective-permute-start | bytes 811016 | tf_op jit(solution)/shard_map/ppermute | solution.py:267
  109.3 0.7 copy-start.4
  109.3 0.8 copy-start.5
  110.1 3.7 %slice-start.1 = ((bf16[1056,128]{1,0:T(8,128)(2,1)}), bf16[1024,128]{1,0:T(8,128)(2,1)S(1)}, s32[]{:S(2)}) async-start(bf16[1056,128]{1,0:T(8,128)(2,1)} %copy-done.5), calls=%async_computation.5 | async-start | bytes 524288 | tf_op jit(solution)/shard_map/slice | solution.py:289
  110.1 3.7 %slice-start = ((bf16[1056,128]{1,0:T(8,128)(2,1)}), bf16[1024,128]{1,0:T(8,128)(2,1)S(1)}, s32[]{:S(2)}) async-start(bf16[1056,128]{1,0:T(8,128)(2,1)} %copy-done.4), calls=%async_computation.4 | async-start | bytes 524288 | tf_op jit(solution)/shard_map/slice | solution.py:289
  110.2 9.1 %collective-permute-start.12 = (bf16[528,128]{1,0:T(8,128)(2,1)S(1)}, bf16[528,128]{1,0:T(8,128)(2,1)S(1)}, u32[]{:S(2)}, u32[]{:S(2)}) collective-permute-start(bf16[528,128]{1,0:T(8,128)(2,1)S(1)} %get-tuple-element.34), channel_id=1, source_target_pairs={{0,4},{4,16},{16,20},{20,0},{1,5},{5,17},{17,21},{21,1},{2,6},{6,1... | collective-permute-start | bytes 405512 | tf_op jit(solution)/shard_map/ppermute | solution.py:267
  110.2 9.0 %collective-permute-start.11 = (bf16[528,128]{1,0:T(8,128)(2,1)S(1)}, bf16[528,128]{1,0:T(8,128)(2,1)S(1)}, u32[]{:S(2)}, u32[]{:S(2)}) collective-permute-start(bf16[528,128]{1,0:T(8,128)(2,1)S(1)} %get-tuple-element.33), channel_id=1, source_target_pairs={{0,16},{4,20},{16,0},{20,4},{1,17},{5,21},{17,1},{21,5},{2,18},{6,... | collective-permute-start | bytes 405512 | tf_op jit(solution)/shard_map/ppermute | solution.py:267
  111.9 7.5 %collective-permute-start.10 = (bf16[528,128]{1,0:T(8,128)(2,1)S(1)}, bf16[528,128]{1,0:T(8,128)(2,1)S(1)}, u32[]{:S(2)}, u32[]{:S(2)}) collective-permute-start(bf16[528,128]{1,0:T(8,128)(2,1)S(1)} %get-tuple-element.32), channel_id=1, source_target_pairs={{0,20},{4,0},{16,4},{20,16},{1,21},{5,1},{17,5},{21,17},{2,22},{6,... | collective-permute-start | bytes 405512 | tf_op jit(solution)/shard_map/ppermute | solution.py:267
  119.3 0.7 copy-start.7
  119.4 0.6 copy-start.6
  120.0 0.9 slice-start.2
  120.0 1.0 slice-start.3

commit v2 on v1

--- a/solution.py
+++ b/solution.py
@@ -182,6 +182,17 @@
             best = jnp.maximum(best, part)
         return best
 
+    def produce_all(t, n, best):
+        keys = k_scr[pl.ds(n * GROUP, GROUP)].reshape(GROUP * KT, 2 * HD)
+        scores = jnp.dot(keys, q_scr[t], preferred_element_type=jnp.float32)
+        for g in range(GROUP):
+            s = scores[g * KT:(g + 1) * KT]
+            s_scr[g] = s
+            for d, bias in enumerate(bias_rows(t, n * GROUP + g)):
+                part = jnp.max(s[d * TOK:(d + 1) * TOK].reshape(TOK // 8, 8, wide), axis=0) + bias
+                best = jnp.maximum(best, part)
+        return best
+
     def consume(t, j, slot, top):
         s = s_scr[slot]
         ps = []
@@ -201,8 +212,11 @@
         for g in range(GROUP):
             j = n * GROUP + g
             p = consume(t, j, g, top)
-            best = produce(t2, n2 * GROUP + g, g, best)
             ps.append(p)
+            if not shared:
+                best = produce(t2, n2 * GROUP + g, g, best)
+        if shared:
+            best = produce_all(t2, n2, best)
         acc_scr[t] = accum + jnp.dot(v_scr[n], jnp.concatenate(ps, axis=0), preferred_element_type=jnp.float32)
         top_scr[t, 0:1, :] = top
         return t2, n2, best, jnp.where(last, FLOOR, top)
@@ -304,8 +318,8 @@
     rest = along_z(after(rest, most))
     mine = [most] + spread(most[:, :2 * TOK])
     q = most[:, 2 * TOK:]
-    qs = [q] + [turn(q, ("yh", "yl"), Y, d) for d in range(1, Y - 1)]
-    qs.append(turn(after(q, qs[1]), ("yh", "yl"), Y, Y - 1))
+    far = turn(q, ("yh", "yl"), Y, 2)
+    qs = [q, turn(q, ("yh", "yl"), Y, 1), far, turn(after(q, far), ("yh", "yl"), Y, 3)]
     mine2 = lax.all_to_all(
         jnp.broadcast_to(rest, (X, *rest.shape)), "x", split_axis=0, concat_axis=0, tiled=True
     )

time: 146 us -> 142 us (0.973)
  Pallas kernels: 39.1 us -> 34.9 us
  blocking collectives: 58.6 us -> 54.9 us
  waiting for transfers between devices: 16.8 us -> 18.6 us
    pallas_call x2, Pallas kernels: 35.1 us -> 30.9 us  [attend(): pl.pallas_call(functools.partial(attend_kernel, shared, planes, join), in...]
    all_to_all x2, blocking collectives: 58.6 us -> 54.9 us  [along_z(): lax.all_to_all(array, ('z', 'c'), split_axis=0, concat_axis=0, tiled=True)]
    ppermute x12, waiting for transfers between devices: 7.92 us -> 9.52 us  [turn(): lax.ppermute(array, axis, [(i, (i + by) % size) for i in range(size)])]
  transfers between devices with their start and end apart: 15 -> 15, of which waited for: 6 -> 5; matrix products, arithmetic and copies ran while one was open for 2% -> 2% of each run, Pallas kernels for 24% -> 22%
where the time goes in v2:
time: 142 us; the launch traced here: 141 us
  blocking collectives  54.9 us (39%)
  Pallas kernels  34.9 us (25%)
  starting transfers between devices  24.3 us (17%)
  waiting for transfers between devices  18.6 us (13%)
  local copies, waits for them, and re-layouts  6.49 us (5%)
    all_to_all x2, blocking collectives, along_z(): lax.all_to_all(array, ('z', 'c'), split_axis=0, concat_axis=0, tiled=True)  54.9 us
    pallas_call x2, Pallas kernels, attend(): pl.pallas_call(functools.partial(attend_kernel, shared, planes, join), in...  30.9 us
    ppermute x12, starting transfers between devices, turn(): lax.ppermute(array, axis, [(i, (i + by) % size) for i in range(size)])  16.3 us
    ppermute x12, waiting for transfers between devices, turn(): lax.ppermute(array, axis, [(i, (i + by) % size) for i in range(size)])  9.52 us
    all_to_all x1, waiting for transfers between devices, along_z(): lax.all_to_all(array, ('z', 'c'), split_axis=0, concat_axis=0, tiled=True)  9.03 us
    all_to_all x1, starting transfers between devices, along_z(): lax.all_to_all(array, ('z', 'c'), split_axis=0, concat_axis=0, tiled=True)  4 us
    all_to_all x1, starting transfers between devices, body(): lax.all_to_all(jnp.broadcast_to(rest, (X, *rest.shape)), 'x', split_axis=...  3.65 us
    unnamed x16, local copies, waits for them, and re-layouts  3.08 us
  transfers between devices with their start and end apart: 15, of which 5 were waited for; matrix products, arithmetic and copies ran while one was open for 2% of the time, Pallas kernels for 22%

profile of v2, /device:TPU:1, one launch (start us, length us, event | category | flops | bytes accessed | tf_op | source)
XLA Modules:
  0.0 140.7 jit_solution(2897706920415687389)
XLA Ops:
  0.0 2.3 %pack.1 = (bf16[16,224,128]{2,1,0:T(8,128)(2,1)}, bf16[16,64,128]{2,1,0:T(8,128)(2,1)}) custom-call(bf16[64,3072]{1,0:T(8,128)(2,1)} %q_ref.1, bf16[64,3072]{1,0:T(8,128)(2,1)} %k_ref.1, bf16[64,3072]{1,0:T(8,128)(2,1)} %v_ref.1), custom_call_target="tpu_custom_call" | custom-call | tf_op jit(solution)/shard_map/pack/pallas_call | solution.py:48
  2.3 35.7 %all_to_all.20.refs_4_ = bf16[16,224,128]{2,1,0:T(8,128)(2,1)S(1)} all-to-all(bf16[16,224,128]{2,1,0:T(8,128)(2,1)} %get-tuple-element.22), channel_id=1, replica_groups=mesh['z'=8,'yh'=2,'c'=2,'yl'=2,'x'=4] {'z','c'}, dimensions={0} | all-to-all | bytes 1835008 | tf_op jit(solution)/shard_map/all_to_all | solution.py:289
  38.0 3.0 %collective-permute-start.1 = (bf16[16,96,128]{2,1,0:T(8,128)(2,1)S(1)}, bf16[16,96,128]{2,1,0:T(8,128)(2,1)S(1)}, u32[]{:S(2)}, u32[]{:S(2)}) collective-permute-start(bf16[16,96,128]{2,1,0:T(8,128)(2,1)S(1)} %slice.168.refs_0_), channel_id=1, source_target_pairs={{0,16},{4,20},{16,0},{20,4},{1,17},{5,21},{17,1},{21,5},{2,18},{6,... | collective-permute-start | bytes 1179656 | tf_op jit(solution)/shard_map/ppermute | solution.py:281
  41.0 0.8 slice.169
  41.8 1.2 collective-permute-start.3
  43.1 2.5 %collective-permute-start.4 = (bf16[16,128,128]{2,1,0:T(8,128)(2,1)}, bf16[16,128,128]{2,1,0:T(8,128)(2,1)}, u32[]{:S(2)}, u32[]{:S(2)}) collective-permute-start(bf16[16,128,128]{2,1,0:T(8,128)(2,1)} %slice.169), channel_id=1, source_target_pairs={{0,2},{1,3},{2,0},{3,1},{4,6},{5,7},{6,4},{7,5},{8,10},{9,11},{10,... | collective-permute-start | bytes 1572872 | tf_op jit(solution)/shard_map/ppermute | solution.py:281
  45.5 1.2 collective-permute-start.5
  46.7 4.0 %all-to-all-start.1 = ((bf16[16,64,128]{2,1,0:T(8,128)(2,1)}), bf16[16,64,128]{2,1,0:T(8,128)(2,1)S(1)}, u32[]{:S(2)}, u32[]{:S(2)}) async-start(bf16[16,64,128]{2,1,0:T(8,128)(2,1)} %get-tuple-element.29), calls=%async_computation.1 | async-start | bytes 524288 | tf_op jit(solution)/shard_map/all_to_all | solution.py:289
  50.7 0.4 collective-permute-start
  51.1 0.0 collective-permute-done.1.refs_2_
  51.1 2.3 %collective-permute-start.2 = (bf16[16,96,128]{2,1,0:T(8,128)(2,1)S(1)}, bf16[16,96,128]{2,1,0:T(8,128)(2,1)}, u32[]{:S(2)}, u32[]{:S(2)}) collective-permute-start(bf16[16,96,128]{2,1,0:T(8,128)(2,1)S(1)} %slice.168.refs_0_), channel_id=1, source_target_pairs={{0,20},{4,0},{16,4},{20,16},{1,21},{5,1},{17,5},{21,17},{2,22},{6,... | collective-permute-start | bytes 1179656 | tf_op jit(solution)/shard_map/ppermute | solution.py:281
  53.4 9.0 %all-to-all-done.1 = bf16[16,64,128]{2,1,0:T(8,128)(2,1)S(1)} async-done(((bf16[16,64,128]{2,1,0:T(8,128)(2,1)}), bf16[16,64,128]{2,1,0:T(8,128)(2,1)S(1)}, u32[]{:S(2)}, u32[]{:S(2)}) %all-to-all-start.1) | async-done | bytes 262176 | tf_op jit(solution)/shard_map/all_to_all | solution.py:289
  62.4 1.2 broadcast_in_dim.2
  63.6 0.0 copy-start.3
  63.6 3.6 %all-to-all-start.2 = ((bf16[4,16,64,128]{3,2,1,0:T(8,128)(2,1)}), bf16[4,16,64,128]{3,2,1,0:T(8,128)(2,1)S(1)}, u32[]{:S(2)}, u32[]{:S(2)}) async-start(bf16[4,16,64,128]{3,2,1,0:T(8,128)(2,1)} %broadcast_in_dim.2), calls=%async_computation.2 | async-start | bytes 2097152 | tf_op jit(solution)/shard_map/all_to_all | solution.py:323
  67.3 0.0 collective-permute-done.refs_1_
  67.3 0.0 collective-permute-done.3.refs_5_
  67.3 2.2 %collective-permute-done.4.refs_6_ = bf16[16,128,128]{2,1,0:T(8,128)(2,1)} collective-permute-done((bf16[16,128,128]{2,1,0:T(8,128)(2,1)}, bf16[16,128,128]{2,1,0:T(8,128)(2,1)}, u32[]{:S(2)}, u32[]{:S(2)}) %collective-permute-start.4) | collective-permute-done | bytes 524320 | tf_op jit(solution)/shard_map/ppermute | solution.py:281
  69.5 0.0 collective-permute-done.5.refs_7_
  69.5 0.0 collective-permute-done.2.refs_3_
  69.5 0.0 copy-done.3
  69.5 19.0 %attend_own.1 = (bf16[1056,128]{1,0:T(8,128)(2,1)S(1)}, bf16[1056,128]{1,0:T(8,128)(2,1)S(1)}, bf16[1056,128]{1,0:T(8,128)(2,1)S(1)}, bf16[1056,128]{1,0:T(8,128)(2,1)S(1)}) custom-call(s32[4]{0:T(128)S(1)} %copy-done.3, bf16[16,96,128]{2,1,0:T(8,128)(2,1)S(1)} %slice.168.refs_0_, bf16[16,96,128]{2,1,0:T(8,128)(2,1)} %collective-permute-done.refs_1_, ...), custom_call_target="tpu_custom_call" | custom-call | flops 17179869184 | bytes 4194304 | tf_op jit(solution)/shard_map/attend_own/pallas_call | solution.py:256
  88.6 0.0 copy-start
  88.6 0.7 copy-done
  89.3 0.7 copy-done.1
  90.0 0.7 copy-done.2
  90.7 0.0 all-to-all-done.2.refs_4_
  90.7 0.4 collective-permute-start.9
  91.1 0.8 collective-permute-start.6
  91.9 1.4 %collective-permute-start.7 = (bf16[1056,128]{1,0:T(8,128)(2,1)}, bf16[1056,128]{1,0:T(8,128)(2,1)S(1)}, u32[]{:S(2)}, u32[]{:S(2)}) collective-permute-start(bf16[1056,128]{1,0:T(8,128)(2,1)} %copy-done.1), channel_id=1, source_target_pairs={{0,16},{4,20},{16,0},{20,4},{1,17},{5,21},{17,1},{21,5},{2,18},{6,... | collective-permute-start | bytes 811016 | tf_op jit(solution)/shard_map/ppermute | solution.py:281
  93.3 0.0 collective-permute-start.8
  93.3 0.1 collective-permute-done.9.refs_5_
  93.4 11.9 %attend_shared.1 = (bf16[528,128]{1,0:T(8,128)(2,1)S(1)}, bf16[528,128]{1,0:T(8,128)(2,1)S(1)}, bf16[528,128]{1,0:T(8,128)(2,1)S(1)}, bf16[528,128]{1,0:T(8,128)(2,1)S(1)}) custom-call(s32[4]{0:T(128)S(1)} %copy-done.3, bf16[16,96,128]{2,1,0:T(8,128)(2,1)S(1)} %slice.168.refs_0_, bf16[16,96,128]{2,1,0:T(8,128)(2,1)} %collective-permute-done.refs_1_, ...), custom_call_target="tpu_custom_call" | custom-call | flops 8589934592 | bytes 4194304 | tf_op jit(solution)/shard_map/attend_shared/pallas_call | solution.py:256
  105.3 0.0 collective-permute-done.6
  105.3 0.0 collective-permute-done.7
  105.3 0.0 copy-start.4
  105.3 2.5 %collective-permute-done.8 = bf16[1056,128]{1,0:T(8,128)(2,1)S(1)} collective-permute-done((bf16[1056,128]{1,0:T(8,128)(2,1)}, bf16[1056,128]{1,0:T(8,128)(2,1)S(1)}, u32[]{:S(2)}, u32[]{:S(2)}) %collective-permute-start.8) | collective-permute-done | bytes 270368 | tf_op jit(solution)/shard_map/ppermute | solution.py:281
  107.8 0.0 copy-done.4
  107.8 0.7 copy-done.5
  108.6 0.0 slice-start.1
  108.6 0.0 slice-start
  108.6 0.1 collective-permute-start.12
  108.7 1.5 %collective-permute-start.11 = (bf16[528,128]{1,0:T(8,128)(2,1)S(1)}, bf16[528,128]{1,0:T(8,128)(2,1)S(1)}, u32[]{:S(2)}, u32[]{:S(2)}) collective-permute-start(bf16[528,128]{1,0:T(8,128)(2,1)S(1)} %get-tuple-element.33), channel_id=1, source_target_pairs={{0,16},{4,20},{16,0},{20,4},{1,17},{5,21},{17,1},{21,5},{2,18},{6,... | collective-permute-start | bytes 405512 | tf_op jit(solution)/shard_map/ppermute | solution.py:281
  110.2 2.0 %collective-permute-start.10 = (bf16[528,128]{1,0:T(8,128)(2,1)S(1)}, bf16[528,128]{1,0:T(8,128)(2,1)S(1)}, u32[]{:S(2)}, u32[]{:S(2)}) collective-permute-start(bf16[528,128]{1,0:T(8,128)(2,1)S(1)} %get-tuple-element.32), channel_id=1, source_target_pairs={{0,20},{4,0},{16,4},{20,16},{1,21},{5,1},{17,5},{21,17},{2,22},{6,... | collective-permute-start | bytes 405512 | tf_op jit(solution)/shard_map/ppermute | solution.py:281
  112.2 0.1 fusion.8
  112.3 0.0 slice-done.1
  112.3 0.0 slice-done
  112.3 0.6 fusion.1
  113.0 4.8 %collective-permute-done.12 = bf16[528,128]{1,0:T(8,128)(2,1)S(1)} collective-permute-done((bf16[528,128]{1,0:T(8,128)(2,1)S(1)}, bf16[528,128]{1,0:T(8,128)(2,1)S(1)}, u32[]{:S(2)}, u32[]{:S(2)}) %collective-permute-start.12) | collective-permute-done | bytes 135200 | tf_op jit(solution)/shard_map/ppermute | solution.py:281
  117.7 0.0 collective-permute-done.11
  117.8 0.0 collective-permute-done.10
  117.8 0.0 copy-start.6
  117.8 0.1 fusion.12
  117.9 0.1 mul.87
  118.0 0.1 mul.90
  118.0 0.1 mul.93
  118.1 0.1 mul.84
  118.2 0.2 copy-done.7
  118.4 0.0 copy-done.6
  118.4 0.9 slice-done.2
  119.3 0.1 slice-done.3
  119.4 0.3 fusion.5
  119.8 19.2 %all_to_all.21.ref = bf16[16,96,128]{2,1,0:T(8,128)(2,1)} all-to-all(bf16[16,96,128]{2,1,0:T(8,128)(2,1)S(1)} %pad_maximum_fusion), channel_id=1, replica_groups=mesh['z'=8,'yh'=2,'c'=2,'yl'=2,'x'=4] {'z','c'}, dimensions={0} | all-to-all | bytes 786432 | tf_op jit(solution)/shard_map/all_to_all | solution.py:289
  139.0 1.7 %unpack.1 = bf16[64,3072]{1,0:T(8,128)(2,1)} custom-call(bf16[16,96,128]{2,1,0:T(8,128)(2,1)} %all_to_all.21.ref), custom_call_target="tpu_custom_call" | custom-call | tf_op jit(solution)/shard_map/unpack/pallas_call | solution.py:72
  (20 shorter events, 0.2 us)
Async XLA Ops:
  38.0 13.1 %collective-permute-start.1 = (bf16[16,96,128]{2,1,0:T(8,128)(2,1)S(1)}, bf16[16,96,128]{2,1,0:T(8,128)(2,1)S(1)}, u32[]{:S(2)}, u32[]{:S(2)}) collective-permute-start(bf16[16,96,128]{2,1,0:T(8,128)(2,1)S(1)} %slice.168.refs_0_), channel_id=1, source_target_pairs={{0,16},{4,20},{16,0},{20,4},{1,17},{5,21},{17,1},{21,5},{2,18},{6,... | collective-permute-start | bytes 1179656 | tf_op jit(solution)/shard_map/ppermute | solution.py:281
  41.8 25.5 %collective-permute-start.3 = (bf16[16,128,128]{2,1,0:T(8,128)(2,1)}, bf16[16,128,128]{2,1,0:T(8,128)(2,1)S(1)}, u32[]{:S(2)}, u32[]{:S(2)}) collective-permute-start(bf16[16,128,128]{2,1,0:T(8,128)(2,1)} %slice.169), channel_id=1, source_target_pairs={{0,1},{1,2},{2,3},{3,0},{4,5},{5,6},{6,7},{7,4},{8,9},{9,10},{10,1... | collective-permute-start | bytes 1572872 | tf_op jit(solution)/shard_map/ppermute | solution.py:281
  43.1 26.5 %collective-permute-start.4 = (bf16[16,128,128]{2,1,0:T(8,128)(2,1)}, bf16[16,128,128]{2,1,0:T(8,128)(2,1)}, u32[]{:S(2)}, u32[]{:S(2)}) collective-permute-start(bf16[16,128,128]{2,1,0:T(8,128)(2,1)} %slice.169), channel_id=1, source_target_pairs={{0,2},{1,3},{2,0},{3,1},{4,6},{5,7},{6,4},{7,5},{8,10},{9,11},{10,... | collective-permute-start | bytes 1572872 | tf_op jit(solution)/shard_map/ppermute | solution.py:281
  45.5 24.0 %collective-permute-start.5 = (bf16[16,128,128]{2,1,0:T(8,128)(2,1)}, bf16[16,128,128]{2,1,0:T(8,128)(2,1)}, u32[]{:S(2)}, u32[]{:S(2)}) collective-permute-start(bf16[16,128,128]{2,1,0:T(8,128)(2,1)} %slice.169), channel_id=1, source_target_pairs={{0,3},{1,0},{2,1},{3,2},{4,7},{5,4},{6,5},{7,6},{8,11},{9,8},{10,9... | collective-permute-start | bytes 1572872 | tf_op jit(solution)/shard_map/ppermute | solution.py:281
  46.7 15.7 %all-to-all-start.1 = ((bf16[16,64,128]{2,1,0:T(8,128)(2,1)}), bf16[16,64,128]{2,1,0:T(8,128)(2,1)S(1)}, u32[]{:S(2)}, u32[]{:S(2)}) async-start(bf16[16,64,128]{2,1,0:T(8,128)(2,1)} %get-tuple-element.29), calls=%async_computation.1 | async-start | bytes 524288 | tf_op jit(solution)/shard_map/all_to_all | solution.py:289
  50.7 16.6 %collective-permute-start = (bf16[16,96,128]{2,1,0:T(8,128)(2,1)S(1)}, bf16[16,96,128]{2,1,0:T(8,128)(2,1)}, u32[]{:S(2)}, u32[]{:S(2)}) collective-permute-start(bf16[16,96,128]{2,1,0:T(8,128)(2,1)S(1)} %slice.168.refs_0_), channel_id=1, source_target_pairs={{0,4},{4,16},{16,20},{20,0},{1,5},{5,17},{17,21},{21,1},{2,6},{6,1... | collective-permute-start | bytes 1179656 | tf_op jit(solution)/shard_map/ppermute | solution.py:281
  51.1 18.5 %collective-permute-start.2 = (bf16[16,96,128]{2,1,0:T(8,128)(2,1)S(1)}, bf16[16,96,128]{2,1,0:T(8,128)(2,1)}, u32[]{:S(2)}, u32[]{:S(2)}) collective-permute-start(bf16[16,96,128]{2,1,0:T(8,128)(2,1)S(1)} %slice.168.refs_0_), channel_id=1, source_target_pairs={{0,20},{4,0},{16,4},{20,16},{1,21},{5,1},{17,5},{21,17},{2,22},{6,... | collective-permute-start | bytes 1179656 | tf_op jit(solution)/shard_map/ppermute | solution.py:281
  63.6 5.9 %copy-start.3 = (s32[4]{0:T(128)S(1)}, s32[4]{0:T(128)}, u32[]{:S(2)}) copy-start(s32[4]{0:T(128)} %span_tiles.3) | copy-start | bytes 52
  63.6 27.1 %all-to-all-start.2 = ((bf16[4,16,64,128]{3,2,1,0:T(8,128)(2,1)}), bf16[4,16,64,128]{3,2,1,0:T(8,128)(2,1)S(1)}, u32[]{:S(2)}, u32[]{:S(2)}) async-start(bf16[4,16,64,128]{3,2,1,0:T(8,128)(2,1)} %broadcast_in_dim.2), calls=%async_computation.2 | async-start | bytes 2097152 | tf_op jit(solution)/shard_map/all_to_all | solution.py:323
  88.6 0.7 copy-start
  89.3 0.7 copy-start.1
  90.0 0.7 copy-start.2
  90.7 2.7 %collective-permute-start.9 = (bf16[4,16,64,128]{3,2,1,0:T(8,128)(2,1)S(1)}, bf16[4,16,64,128]{3,2,1,0:T(8,128)(2,1)S(1)}, u32[]{:S(2)}, u32[]{:S(2)}) collective-permute-start(bf16[4,16,64,128]{3,2,1,0:T(8,128)(2,1)S(1)} %all-to-all-done.2.refs_4_), channel_id=1, source_target_pairs={{0,8},{8,0},{1,9},{9,1},{2,10},{10,2},{3,11},{11,3},{4,12},{12,4},... | collective-permute-start | bytes 3145736 | tf_op jit(solution)/shard_map/ppermute | solution.py:327
  91.1 14.2 %collective-permute-start.6 = (bf16[1056,128]{1,0:T(8,128)(2,1)}, bf16[1056,128]{1,0:T(8,128)(2,1)S(1)}, u32[]{:S(2)}, u32[]{:S(2)}) collective-permute-start(bf16[1056,128]{1,0:T(8,128)(2,1)} %copy-done.2), channel_id=1, source_target_pairs={{0,20},{4,0},{16,4},{20,16},{1,21},{5,1},{17,5},{21,17},{2,22},{6,... | collective-permute-start | bytes 811016 | tf_op jit(solution)/shard_map/ppermute | solution.py:281
  91.9 13.4 %collective-permute-start.7 = (bf16[1056,128]{1,0:T(8,128)(2,1)}, bf16[1056,128]{1,0:T(8,128)(2,1)S(1)}, u32[]{:S(2)}, u32[]{:S(2)}) collective-permute-start(bf16[1056,128]{1,0:T(8,128)(2,1)} %copy-done.1), channel_id=1, source_target_pairs={{0,16},{4,20},{16,0},{20,4},{1,17},{5,21},{17,1},{21,5},{2,18},{6,... | collective-permute-start | bytes 811016 | tf_op jit(solution)/shard_map/ppermute | solution.py:281
  93.3 14.5 %collective-permute-start.8 = (bf16[1056,128]{1,0:T(8,128)(2,1)}, bf16[1056,128]{1,0:T(8,128)(2,1)S(1)}, u32[]{:S(2)}, u32[]{:S(2)}) collective-permute-start(bf16[1056,128]{1,0:T(8,128)(2,1)} %copy-done), channel_id=1, source_target_pairs={{0,4},{4,16},{16,20},{20,0},{1,5},{5,17},{17,21},{21,1},{2,6},{6,1... | collective-permute-start | bytes 811016 | tf_op jit(solution)/shard_map/ppermute | solution.py:281
  105.3 2.5 %copy-start.4 = (bf16[1056,128]{1,0:T(8,128)(2,1)}, bf16[1056,128]{1,0:T(8,128)(2,1)S(1)}, u32[]{:S(2)}) copy-start(bf16[1056,128]{1,0:T(8,128)(2,1)S(1)} %collective-permute-done.7) | copy-start | bytes 811012
  107.8 0.7 copy-start.5
  108.6 3.8 %slice-start.1 = ((bf16[1056,128]{1,0:T(8,128)(2,1)}), bf16[1024,128]{1,0:T(8,128)(2,1)S(1)}, s32[]{:S(2)}) async-start(bf16[1056,128]{1,0:T(8,128)(2,1)} %copy-done.5), calls=%async_computation.5 | async-start | bytes 524288 | tf_op jit(solution)/shard_map/slice | solution.py:303
  108.6 3.7 %slice-start = ((bf16[1056,128]{1,0:T(8,128)(2,1)}), bf16[1024,128]{1,0:T(8,128)(2,1)S(1)}, s32[]{:S(2)}) async-start(bf16[1056,128]{1,0:T(8,128)(2,1)} %copy-done.4), calls=%async_computation.4 | async-start | bytes 524288 | tf_op jit(solution)/shard_map/slice | solution.py:303
  108.6 9.1 %collective-permute-start.12 = (bf16[528,128]{1,0:T(8,128)(2,1)S(1)}, bf16[528,128]{1,0:T(8,128)(2,1)S(1)}, u32[]{:S(2)}, u32[]{:S(2)}) collective-permute-start(bf16[528,128]{1,0:T(8,128)(2,1)S(1)} %get-tuple-element.34), channel_id=1, source_target_pairs={{0,4},{4,16},{16,20},{20,0},{1,5},{5,17},{17,21},{21,1},{2,6},{6,1... | collective-permute-start | bytes 405512 | tf_op jit(solution)/shard_map/ppermute | solution.py:281
  108.7 9.0 %collective-permute-start.11 = (bf16[528,128]{1,0:T(8,128)(2,1)S(1)}, bf16[528,128]{1,0:T(8,128)(2,1)S(1)}, u32[]{:S(2)}, u32[]{:S(2)}) collective-permute-start(bf16[528,128]{1,0:T(8,128)(2,1)S(1)} %get-tuple-element.33), channel_id=1, source_target_pairs={{0,16},{4,20},{16,0},{20,4},{1,17},{5,21},{17,1},{21,5},{2,18},{6,... | collective-permute-start | bytes 405512 | tf_op jit(solution)/shard_map/ppermute | solution.py:281
  110.2 7.6 %collective-permute-start.10 = (bf16[528,128]{1,0:T(8,128)(2,1)S(1)}, bf16[528,128]{1,0:T(8,128)(2,1)S(1)}, u32[]{:S(2)}, u32[]{:S(2)}) collective-permute-start(bf16[528,128]{1,0:T(8,128)(2,1)S(1)} %get-tuple-element.32), channel_id=1, source_target_pairs={{0,20},{4,0},{16,4},{20,16},{1,21},{5,1},{17,5},{21,17},{2,22},{6,... | collective-permute-start | bytes 405512 | tf_op jit(solution)/shard_map/ppermute | solution.py:281
  117.7 0.7 copy-start.7
  117.8 0.7 copy-start.6
  118.4 0.9 slice-start.2
  118.4 1.0 slice-start.3

commit v3 on v2

--- a/solution.py
+++ b/solution.py
@@ -17,7 +17,7 @@
 HEADS_HERE = 3
 QT = Y * TOK
 KT = X * TOK
-PLANES = 4
+PLANES = 2
 CHUNKS = Z * CORES
 GROUP = 4
 VROWS = HD + 16
@@ -311,7 +311,8 @@
         return [turn(array, "x", X, d) for d in range(1, X)]
 
     def exchange(out):
-        return [out[0]] + [turn(out[d], ("yh", "yl"), Y, -d) for d in range(1, Y)]
+        far = turn(out[2], ("yh", "yl"), Y, -2)
+        return [out[0], far] + [turn(out[d], ("yh", "yl"), Y, -d) for d in (1, 3)]
 
     most, rest = pack(queries, keys, values)
     most = along_z(most)

time: 142 us -> 145 us (1.021)
  Pallas kernels: 34.9 us -> 41.3 us
  waiting for transfers between devices: 18.6 us -> 17 us
  starting transfers between devices: 24.3 us -> 22.8 us
    pallas_call x2, Pallas kernels: 30.9 us -> 34.7 us  [attend(): pl.pallas_call(functools.partial(attend_kernel, shared, planes, join), in...]
    ppermute x12, waiting for transfers between devices: 9.52 us -> 7.21 us  [turn(): lax.ppermute(array, axis, [(i, (i + by) % size) for i in range(size)])]
    ppermute x12, starting transfers between devices: 16.3 us -> 14.8 us  [turn(): lax.ppermute(array, axis, [(i, (i + by) % size) for i in range(size)])]
  transfers between devices with their start and end apart: 15 -> 15, of which waited for: 5 -> 7; matrix products, arithmetic and copies ran while one was open for 2% -> 2% of each run, Pallas kernels for 22% -> 24%
where the time goes in v3:
time: 145 us
  blocking collectives  55.5 us (38%)
  Pallas kernels  41.3 us (28%)
  starting transfers between devices  22.8 us (16%)
  waiting for transfers between devices  17 us (12%)
  local copies, waits for them, and re-layouts  6.49 us (4%)
    all_to_all x2, blocking collectives, along_z(): lax.all_to_all(array, ('z', 'c'), split_axis=0, concat_axis=0, tiled=True)  55.5 us
    pallas_call x2, Pallas kernels, attend(): pl.pallas_call(functools.partial(attend_kernel, shared, planes, join), in...  34.7 us
    ppermute x12, starting transfers between devices, turn(): lax.ppermute(array, axis, [(i, (i + by) % size) for i in range(size)])  14.8 us
    all_to_all x1, waiting for transfers between devices, along_z(): lax.all_to_all(array, ('z', 'c'), split_axis=0, concat_axis=0, tiled=True)  9.03 us
    ppermute x12, waiting for transfers between devices, turn(): lax.ppermute(array, axis, [(i, (i + by) % size) for i in range(size)])  7.21 us
    all_to_all x1, starting transfers between devices, along_z(): lax.all_to_all(array, ('z', 'c'), split_axis=0, concat_axis=0, tiled=True)  4 us
    all_to_all x1, starting transfers between devices, body(): lax.all_to_all(jnp.broadcast_to(rest, (X, *rest.shape)), 'x', split_axis=...  3.65 us
    pallas_call x1, Pallas kernels, pack(): pl.pallas_call(pack_kernel, grid=(Z // PLANES,), in_specs=[pl.BlockSpec((...  3.52 us
  transfers between devices with their start and end apart: 15, of which 7 were waited for; matrix products, arithmetic and copies ran while one was open for 2% of the time, Pallas kernels for 24%

profile of v3, /device:TPU:1, one launch (start us, length us, event | category | flops | bytes accessed | tf_op | source)
XLA Modules:
  0.0 144.6 jit_solution(4482333232196423037)
XLA Ops:
  0.0 3.5 %pack.1 = (bf16[16,224,128]{2,1,0:T(8,128)(2,1)}, bf16[16,64,128]{2,1,0:T(8,128)(2,1)}) custom-call(bf16[64,3072]{1,0:T(8,128)(2,1)} %q_ref.1, bf16[64,3072]{1,0:T(8,128)(2,1)} %k_ref.1, bf16[64,3072]{1,0:T(8,128)(2,1)} %v_ref.1), custom_call_target="tpu_custom_call" | custom-call | tf_op jit(solution)/shard_map/pack/pallas_call | solution.py:48
  3.5 35.7 %all_to_all.20.refs_4_ = bf16[16,224,128]{2,1,0:T(8,128)(2,1)S(1)} all-to-all(bf16[16,224,128]{2,1,0:T(8,128)(2,1)} %get-tuple-element.22), channel_id=1, replica_groups=mesh['z'=8,'yh'=2,'c'=2,'yl'=2,'x'=4] {'z','c'}, dimensions={0} | all-to-all | bytes 1835008 | tf_op jit(solution)/shard_map/all_to_all | solution.py:289
  39.3 3.0 %collective-permute-start.1 = (bf16[16,96,128]{2,1,0:T(8,128)(2,1)S(1)}, bf16[16,96,128]{2,1,0:T(8,128)(2,1)S(1)}, u32[]{:S(2)}, u32[]{:S(2)}) collective-permute-start(bf16[16,96,128]{2,1,0:T(8,128)(2,1)S(1)} %slice.168.refs_0_), channel_id=1, source_target_pairs={{0,16},{4,20},{16,0},{20,4},{1,17},{5,21},{17,1},{21,5},{2,18},{6,... | collective-permute-start | bytes 1179656 | tf_op jit(solution)/shard_map/ppermute | solution.py:281
  42.3 0.8 slice.169
  43.1 1.2 collective-permute-start.3
  44.3 2.5 %collective-permute-start.4 = (bf16[16,128,128]{2,1,0:T(8,128)(2,1)}, bf16[16,128,128]{2,1,0:T(8,128)(2,1)}, u32[]{:S(2)}, u32[]{:S(2)}) collective-permute-start(bf16[16,128,128]{2,1,0:T(8,128)(2,1)} %slice.169), channel_id=1, source_target_pairs={{0,2},{1,3},{2,0},{3,1},{4,6},{5,7},{6,4},{7,5},{8,10},{9,11},{10,... | collective-permute-start | bytes 1572872 | tf_op jit(solution)/shard_map/ppermute | solution.py:281
  46.8 1.2 collective-permute-start.5
  48.0 4.0 %all-to-all-start.1 = ((bf16[16,64,128]{2,1,0:T(8,128)(2,1)}), bf16[16,64,128]{2,1,0:T(8,128)(2,1)S(1)}, u32[]{:S(2)}, u32[]{:S(2)}) async-start(bf16[16,64,128]{2,1,0:T(8,128)(2,1)} %get-tuple-element.29), calls=%async_computation.1 | async-start | bytes 524288 | tf_op jit(solution)/shard_map/all_to_all | solution.py:289
  52.0 0.4 collective-permute-start
  52.4 0.0 collective-permute-done.1.refs_2_
  52.4 2.3 %collective-permute-start.2 = (bf16[16,96,128]{2,1,0:T(8,128)(2,1)S(1)}, bf16[16,96,128]{2,1,0:T(8,128)(2,1)}, u32[]{:S(2)}, u32[]{:S(2)}) collective-permute-start(bf16[16,96,128]{2,1,0:T(8,128)(2,1)S(1)} %slice.168.refs_0_), channel_id=1, source_target_pairs={{0,20},{4,0},{16,4},{20,16},{1,21},{5,1},{17,5},{21,17},{2,22},{6,... | collective-permute-start | bytes 1179656 | tf_op jit(solution)/shard_map/ppermute | solution.py:281
  54.6 9.0 %all-to-all-done.1 = bf16[16,64,128]{2,1,0:T(8,128)(2,1)S(1)} async-done(((bf16[16,64,128]{2,1,0:T(8,128)(2,1)}), bf16[16,64,128]{2,1,0:T(8,128)(2,1)S(1)}, u32[]{:S(2)}, u32[]{:S(2)}) %all-to-all-start.1) | async-done | bytes 262176 | tf_op jit(solution)/shard_map/all_to_all | solution.py:289
  63.7 1.2 broadcast_in_dim.2
  64.9 0.0 copy-start.3
  64.9 3.6 %all-to-all-start.2 = ((bf16[4,16,64,128]{3,2,1,0:T(8,128)(2,1)}), bf16[4,16,64,128]{3,2,1,0:T(8,128)(2,1)S(1)}, u32[]{:S(2)}, u32[]{:S(2)}) async-start(bf16[4,16,64,128]{3,2,1,0:T(8,128)(2,1)} %broadcast_in_dim.2), calls=%async_computation.2 | async-start | bytes 2097152 | tf_op jit(solution)/shard_map/all_to_all | solution.py:324
  68.6 0.0 collective-permute-done.refs_1_
  68.6 0.0 collective-permute-done.3.refs_5_
  68.6 2.2 %collective-permute-done.4.refs_6_ = bf16[16,128,128]{2,1,0:T(8,128)(2,1)} collective-permute-done((bf16[16,128,128]{2,1,0:T(8,128)(2,1)}, bf16[16,128,128]{2,1,0:T(8,128)(2,1)}, u32[]{:S(2)}, u32[]{:S(2)}) %collective-permute-start.4) | collective-permute-done | bytes 524320 | tf_op jit(solution)/shard_map/ppermute | solution.py:281
  70.8 0.0 collective-permute-done.5.refs_7_
  70.8 0.0 collective-permute-done.2.refs_3_
  70.8 0.0 copy-done.3
  70.8 21.5 %attend_own.1 = (bf16[1056,128]{1,0:T(8,128)(2,1)S(1)}, bf16[1056,128]{1,0:T(8,128)(2,1)S(1)}, bf16[1056,128]{1,0:T(8,128)(2,1)S(1)}, bf16[1056,128]{1,0:T(8,128)(2,1)S(1)}) custom-call(s32[4]{0:T(128)S(1)} %copy-done.3, bf16[16,96,128]{2,1,0:T(8,128)(2,1)S(1)} %slice.168.refs_0_, bf16[16,96,128]{2,1,0:T(8,128)(2,1)} %collective-permute-done.refs_1_, ...), custom_call_target="tpu_custom_call" | custom-call | flops 17179869184 | bytes 4194304 | tf_op jit(solution)/shard_map/attend_own/pallas_call | solution.py:256
  92.3 0.0 copy-start
  92.3 0.7 copy-done
  93.0 0.0 copy-start.1
  93.0 0.7 copy-done.1
  93.7 0.7 copy-done.2
  94.4 0.0 all-to-all-done.2.refs_4_
  94.4 0.4 collective-permute-start.9
  94.8 0.0 collective-permute-start.6
  94.8 0.4 collective-permute-start.7
  95.2 1.1 collective-permute-start.8
  96.3 0.8 collective-permute-done.9.refs_5_
  97.1 13.2 %attend_shared.1 = (bf16[528,128]{1,0:T(8,128)(2,1)S(1)}, bf16[528,128]{1,0:T(8,128)(2,1)S(1)}, bf16[528,128]{1,0:T(8,128)(2,1)S(1)}, bf16[528,128]{1,0:T(8,128)(2,1)S(1)}) custom-call(s32[4]{0:T(128)S(1)} %copy-done.3, bf16[16,96,128]{2,1,0:T(8,128)(2,1)S(1)} %slice.168.refs_0_, bf16[16,96,128]{2,1,0:T(8,128)(2,1)} %collective-permute-done.refs_1_, ...), custom_call_target="tpu_custom_call" | custom-call | flops 8589934592 | bytes 4194304 | tf_op jit(solution)/shard_map/attend_shared/pallas_call | solution.py:256
  110.3 0.0 collective-permute-done.6
  110.3 0.0 collective-permute-done.7
  110.4 0.0 copy-start.4
  110.4 0.4 collective-permute-done.8
  110.8 0.3 copy-done.4
  111.1 0.4 copy-done.5
  111.5 0.0 slice-start.1
  111.6 0.0 slice-start
  111.6 0.1 collective-permute-start.12
  111.7 2.7 %collective-permute-start.11 = (bf16[528,128]{1,0:T(8,128)(2,1)S(1)}, bf16[528,128]{1,0:T(8,128)(2,1)S(1)}, u32[]{:S(2)}, u32[]{:S(2)}) collective-permute-start(bf16[528,128]{1,0:T(8,128)(2,1)S(1)} %get-tuple-element.32), channel_id=1, source_target_pairs={{0,20},{4,0},{16,4},{20,16},{1,21},{5,1},{17,5},{21,17},{2,22},{6,... | collective-permute-start | bytes 405512 | tf_op jit(solution)/shard_map/ppermute | solution.py:281
  114.3 0.0 collective-permute-start.10
  114.3 0.1 fusion.8
  114.5 0.0 slice-done.1
  114.5 0.0 slice-done
  114.5 0.6 fusion.1
  115.1 2.4 %collective-permute-done.12 = bf16[528,128]{1,0:T(8,128)(2,1)S(1)} collective-permute-done((bf16[528,128]{1,0:T(8,128)(2,1)S(1)}, bf16[528,128]{1,0:T(8,128)(2,1)S(1)}, u32[]{:S(2)}, u32[]{:S(2)}) %collective-permute-start.12) | collective-permute-done | bytes 135200 | tf_op jit(solution)/shard_map/ppermute | solution.py:281
  117.5 2.0 %collective-permute-done.11 = bf16[528,128]{1,0:T(8,128)(2,1)S(1)} collective-permute-done((bf16[528,128]{1,0:T(8,128)(2,1)S(1)}, bf16[528,128]{1,0:T(8,128)(2,1)S(1)}, u32[]{:S(2)}, u32[]{:S(2)}) %collective-permute-start.11) | collective-permute-done | bytes 135200 | tf_op jit(solution)/shard_map/ppermute | solution.py:281
  119.6 0.1 collective-permute-done.10
  119.7 0.1 fusion.12
  119.8 0.1 mul.87
  119.9 0.1 mul.90
  119.9 0.1 mul.93
  120.0 0.1 mul.84
  120.1 0.1 copy-done.7
  120.2 0.1 copy-done.6
  120.3 0.9 slice-done.2
  121.2 0.1 slice-done.3
  121.3 0.3 fusion.5
  121.7 19.8 %all_to_all.21.ref = bf16[16,96,128]{2,1,0:T(8,128)(2,1)} all-to-all(bf16[16,96,128]{2,1,0:T(8,128)(2,1)S(1)} %pad_maximum_fusion), channel_id=1, replica_groups=mesh['z'=8,'yh'=2,'c'=2,'yl'=2,'x'=4] {'z','c'}, dimensions={0} | all-to-all | bytes 786432 | tf_op jit(solution)/shard_map/all_to_all | solution.py:289
  141.5 3.1 %unpack.1 = bf16[64,3072]{1,0:T(8,128)(2,1)} custom-call(bf16[16,96,128]{2,1,0:T(8,128)(2,1)} %all_to_all.21.ref), custom_call_target="tpu_custom_call" | custom-call | tf_op jit(solution)/shard_map/unpack/pallas_call | solution.py:72
  (20 shorter events, 0.2 us)
Async XLA Ops:
  39.3 13.1 %collective-permute-start.1 = (bf16[16,96,128]{2,1,0:T(8,128)(2,1)S(1)}, bf16[16,96,128]{2,1,0:T(8,128)(2,1)S(1)}, u32[]{:S(2)}, u32[]{:S(2)}) collective-permute-start(bf16[16,96,128]{2,1,0:T(8,128)(2,1)S(1)} %slice.168.refs_0_), channel_id=1, source_target_pairs={{0,16},{4,20},{16,0},{20,4},{1,17},{5,21},{17,1},{21,5},{2,18},{6,... | collective-permute-start | bytes 1179656 | tf_op jit(solution)/shard_map/ppermute | solution.py:281
  43.1 25.5 %collective-permute-start.3 = (bf16[16,128,128]{2,1,0:T(8,128)(2,1)}, bf16[16,128,128]{2,1,0:T(8,128)(2,1)S(1)}, u32[]{:S(2)}, u32[]{:S(2)}) collective-permute-start(bf16[16,128,128]{2,1,0:T(8,128)(2,1)} %slice.169), channel_id=1, source_target_pairs={{0,1},{1,2},{2,3},{3,0},{4,5},{5,6},{6,7},{7,4},{8,9},{9,10},{10,1... | collective-permute-start | bytes 1572872 | tf_op jit(solution)/shard_map/ppermute | solution.py:281
  44.3 26.5 %collective-permute-start.4 = (bf16[16,128,128]{2,1,0:T(8,128)(2,1)}, bf16[16,128,128]{2,1,0:T(8,128)(2,1)}, u32[]{:S(2)}, u32[]{:S(2)}) collective-permute-start(bf16[16,128,128]{2,1,0:T(8,128)(2,1)} %slice.169), channel_id=1, source_target_pairs={{0,2},{1,3},{2,0},{3,1},{4,6},{5,7},{6,4},{7,5},{8,10},{9,11},{10,... | collective-permute-start | bytes 1572872 | tf_op jit(solution)/shard_map/ppermute | solution.py:281
  46.8 24.0 %collective-permute-start.5 = (bf16[16,128,128]{2,1,0:T(8,128)(2,1)}, bf16[16,128,128]{2,1,0:T(8,128)(2,1)}, u32[]{:S(2)}, u32[]{:S(2)}) collective-permute-start(bf16[16,128,128]{2,1,0:T(8,128)(2,1)} %slice.169), channel_id=1, source_target_pairs={{0,3},{1,0},{2,1},{3,2},{4,7},{5,4},{6,5},{7,6},{8,11},{9,8},{10,9... | collective-permute-start | bytes 1572872 | tf_op jit(solution)/shard_map/ppermute | solution.py:281
  48.0 15.7 %all-to-all-start.1 = ((bf16[16,64,128]{2,1,0:T(8,128)(2,1)}), bf16[16,64,128]{2,1,0:T(8,128)(2,1)S(1)}, u32[]{:S(2)}, u32[]{:S(2)}) async-start(bf16[16,64,128]{2,1,0:T(8,128)(2,1)} %get-tuple-element.29), calls=%async_computation.1 | async-start | bytes 524288 | tf_op jit(solution)/shard_map/all_to_all | solution.py:289
  52.0 16.6 %collective-permute-start = (bf16[16,96,128]{2,1,0:T(8,128)(2,1)S(1)}, bf16[16,96,128]{2,1,0:T(8,128)(2,1)}, u32[]{:S(2)}, u32[]{:S(2)}) collective-permute-start(bf16[16,96,128]{2,1,0:T(8,128)(2,1)S(1)} %slice.168.refs_0_), channel_id=1, source_target_pairs={{0,4},{4,16},{16,20},{20,0},{1,5},{5,17},{17,21},{21,1},{2,6},{6,1... | collective-permute-start | bytes 1179656 | tf_op jit(solution)/shard_map/ppermute | solution.py:281
  52.4 18.5 %collective-permute-start.2 = (bf16[16,96,128]{2,1,0:T(8,128)(2,1)S(1)}, bf16[16,96,128]{2,1,0:T(8,128)(2,1)}, u32[]{:S(2)}, u32[]{:S(2)}) collective-permute-start(bf16[16,96,128]{2,1,0:T(8,128)(2,1)S(1)} %slice.168.refs_0_), channel_id=1, source_target_pairs={{0,20},{4,0},{16,4},{20,16},{1,21},{5,1},{17,5},{21,17},{2,22},{6,... | collective-permute-start | bytes 1179656 | tf_op jit(solution)/shard_map/ppermute | solution.py:281
  64.9 5.9 %copy-start.3 = (s32[4]{0:T(128)S(1)}, s32[4]{0:T(128)}, u32[]{:S(2)}) copy-start(s32[4]{0:T(128)} %span_tiles.3) | copy-start | bytes 52
  64.9 29.5 %all-to-all-start.2 = ((bf16[4,16,64,128]{3,2,1,0:T(8,128)(2,1)}), bf16[4,16,64,128]{3,2,1,0:T(8,128)(2,1)S(1)}, u32[]{:S(2)}, u32[]{:S(2)}) async-start(bf16[4,16,64,128]{3,2,1,0:T(8,128)(2,1)} %broadcast_in_dim.2), calls=%async_computation.2 | async-start | bytes 2097152 | tf_op jit(solution)/shard_map/all_to_all | solution.py:324
  92.3 0.7 copy-start
  93.0 0.7 copy-start.1
  93.7 0.7 copy-start.2
  94.4 2.7 %collective-permute-start.9 = (bf16[4,16,64,128]{3,2,1,0:T(8,128)(2,1)S(1)}, bf16[4,16,64,128]{3,2,1,0:T(8,128)(2,1)S(1)}, u32[]{:S(2)}, u32[]{:S(2)}) collective-permute-start(bf16[4,16,64,128]{3,2,1,0:T(8,128)(2,1)S(1)} %all-to-all-done.2.refs_4_), channel_id=1, source_target_pairs={{0,8},{8,0},{1,9},{9,1},{2,10},{10,2},{3,11},{11,3},{4,12},{12,4},... | collective-permute-start | bytes 3145736 | tf_op jit(solution)/shard_map/ppermute | solution.py:328
  94.8 15.5 %collective-permute-start.6 = (bf16[1056,128]{1,0:T(8,128)(2,1)}, bf16[1056,128]{1,0:T(8,128)(2,1)S(1)}, u32[]{:S(2)}, u32[]{:S(2)}) collective-permute-start(bf16[1056,128]{1,0:T(8,128)(2,1)} %copy-done.2), channel_id=1, source_target_pairs={{0,16},{4,20},{16,0},{20,4},{1,17},{5,21},{17,1},{21,5},{2,18},{6,... | collective-permute-start | bytes 811016 | tf_op jit(solution)/shard_map/ppermute | solution.py:281
  94.8 15.5 %collective-permute-start.7 = (bf16[1056,128]{1,0:T(8,128)(2,1)}, bf16[1056,128]{1,0:T(8,128)(2,1)S(1)}, u32[]{:S(2)}, u32[]{:S(2)}) collective-permute-start(bf16[1056,128]{1,0:T(8,128)(2,1)} %copy-done.1), channel_id=1, source_target_pairs={{0,20},{4,0},{16,4},{20,16},{1,21},{5,1},{17,5},{21,17},{2,22},{6,... | collective-permute-start | bytes 811016 | tf_op jit(solution)/shard_map/ppermute | solution.py:281
  95.2 15.6 %collective-permute-start.8 = (bf16[1056,128]{1,0:T(8,128)(2,1)}, bf16[1056,128]{1,0:T(8,128)(2,1)S(1)}, u32[]{:S(2)}, u32[]{:S(2)}) collective-permute-start(bf16[1056,128]{1,0:T(8,128)(2,1)} %copy-done), channel_id=1, source_target_pairs={{0,4},{4,16},{16,20},{20,0},{1,5},{5,17},{17,21},{21,1},{2,6},{6,1... | collective-permute-start | bytes 811016 | tf_op jit(solution)/shard_map/ppermute | solution.py:281
  110.4 0.7 copy-start.4
  110.8 0.7 copy-start.5
  111.5 2.9 %slice-start.1 = ((bf16[1056,128]{1,0:T(8,128)(2,1)}), bf16[1024,128]{1,0:T(8,128)(2,1)S(1)}, s32[]{:S(2)}) async-start(bf16[1056,128]{1,0:T(8,128)(2,1)} %copy-done.5), calls=%async_computation.5 | async-start | bytes 524288 | tf_op jit(solution)/shard_map/slice | solution.py:303
  111.6 2.9 %slice-start = ((bf16[1056,128]{1,0:T(8,128)(2,1)}), bf16[1024,128]{1,0:T(8,128)(2,1)S(1)}, s32[]{:S(2)}) async-start(bf16[1056,128]{1,0:T(8,128)(2,1)} %copy-done.4), calls=%async_computation.4 | async-start | bytes 524288 | tf_op jit(solution)/shard_map/slice | solution.py:303
  111.6 6.0 %collective-permute-start.12 = (bf16[528,128]{1,0:T(8,128)(2,1)S(1)}, bf16[528,128]{1,0:T(8,128)(2,1)S(1)}, u32[]{:S(2)}, u32[]{:S(2)}) collective-permute-start(bf16[528,128]{1,0:T(8,128)(2,1)S(1)} %get-tuple-element.34), channel_id=1, source_target_pairs={{0,4},{4,16},{16,20},{20,0},{1,5},{5,17},{17,21},{21,1},{2,6},{6,1... | collective-permute-start | bytes 405512 | tf_op jit(solution)/shard_map/ppermute | solution.py:281
  111.7 7.9 %collective-permute-start.11 = (bf16[528,128]{1,0:T(8,128)(2,1)S(1)}, bf16[528,128]{1,0:T(8,128)(2,1)S(1)}, u32[]{:S(2)}, u32[]{:S(2)}) collective-permute-start(bf16[528,128]{1,0:T(8,128)(2,1)S(1)} %get-tuple-element.32), channel_id=1, source_target_pairs={{0,20},{4,0},{16,4},{20,16},{1,21},{5,1},{17,5},{21,17},{2,22},{6,... | collective-permute-start | bytes 405512 | tf_op jit(solution)/shard_map/ppermute | solution.py:281
  114.3 5.4 %collective-permute-start.10 = (bf16[528,128]{1,0:T(8,128)(2,1)S(1)}, bf16[528,128]{1,0:T(8,128)(2,1)S(1)}, u32[]{:S(2)}, u32[]{:S(2)}) collective-permute-start(bf16[528,128]{1,0:T(8,128)(2,1)S(1)} %get-tuple-element.33), channel_id=1, source_target_pairs={{0,16},{4,20},{16,0},{20,4},{1,17},{5,21},{17,1},{21,5},{2,18},{6,... | collective-permute-start | bytes 405512 | tf_op jit(solution)/shard_map/ppermute | solution.py:281
  119.6 0.7 copy-start.7
  119.7 0.6 copy-start.6
  120.3 0.9 slice-start.2
  120.3 1.0 slice-start.3
